TPU v7x, 128 devices: a whole 4x4x4 slice. The times are simulated.
128 devices in a mesh: section: 8 (over z, y_hi), dp: 16 (over x, y_lo, core).
Axes of the slice: x: 4, y: 4 (y_hi: 2, y_lo: 2; y = y_hi * 2 + y_lo), z: 4, core: 2. Of those that a mesh axis runs over, the one named last changes fastest.
Arguments:
- inputs: bfloat16 [4, 1024, 2560], P(None, 'dp'), may hold values from -6 to 6
- cotangent: bfloat16 [4, 1024, 2560], P(None, 'dp'), may hold values from -6 to 6
- weight: bfloat16 [8, 2560, 2560], P('section'), may hold values from -0.125 to 0.125
- gain: float32 [8, 2560], P('section'), may hold values from 0.1 to 1.9
Outputs:
- acts: bfloat16 [8, 4, 1024, 2560], P('section', None, 'dp')
- input_grads: bfloat16 [8, 4, 1024, 2560], P('section', None, 'dp')
- weight_grad: float32 [8, 2560, 2560], P('section', 'dp')
All inputs are finite; a program needn't handle non-finite values.
Results may differ from a plain program's by a relative error of at most 0.029.
Values may be sent and summed in bfloat16 or wider, within the bound.
A program may use at most 128 MiB of HBM per device.

v0:
```python
import jax
import jax.numpy as jnp
from jax import lax
from jax.sharding import PartitionSpec as P

EPS = 1e-05


def passed_along(array, axis, by):
    size = lax.axis_size(axis)
    pairs = [(i, i + by) for i in range(size) if 0 <= i + by < size]
    return lax.ppermute(array, axis, pairs)


def norm_parts(x, g):
    xf = x.astype(jnp.float32)
    r = lax.rsqrt(jnp.mean(xf * xf, -1, keepdims=True) + EPS)
    n = (xf * r * g).astype(jnp.bfloat16)
    return (xf, r, n)


def silu_slope(a):
    s = jax.nn.sigmoid(a)
    return s * (1.0 + a * (1.0 - s))


def put_row(buffer, value, index):
    return lax.dynamic_update_index_in_dim(buffer, value, index, 0)


def take_row(buffer, index):
    return lax.dynamic_index_in_dim(buffer, index, 0, keepdims=False)


def body(inputs, cotangent, weight, gain):
    sections = lax.axis_size("section")
    section_idx = lax.axis_index("section")
    micro, rows, width = inputs.shape
    w_local = weight[0]
    g_local = gain[0]
    ticks = micro + sections - 1
    zero_rows = jnp.zeros((rows, width), jnp.bfloat16)
    pre_shape = (micro, rows, width)

    def forward_tick(t, carry):
        incoming, saved_in, saved_pre, outputs = carry
        step_m = t - section_idx
        valid = (step_m >= 0) & (step_m < micro)
        index = jnp.clip(step_m, 0, micro - 1)
        x_now = jnp.where(section_idx == 0, take_row(inputs, index), incoming)

        def forward_active(state):
            keep_in, keep_pre, keep_out = state
            xf, r, n = norm_parts(x_now, g_local)
            a = jnp.dot(n, w_local, preferred_element_type=jnp.float32)
            y = (xf + jax.nn.silu(a)).astype(jnp.bfloat16)
            keep_pre = put_row(keep_pre, a, index)
            return (y, (put_row(keep_in, x_now, index), keep_pre, put_row(keep_out, y, index)))

        def forward_passive(state):
            return (zero_rows, state)

        y, state = lax.cond(valid, forward_active, forward_passive, (saved_in, saved_pre, outputs))
        sent = passed_along(y, "section", 1)
        return (sent,) + state

    start = (
        zero_rows,
        jnp.zeros((micro, rows, width), jnp.bfloat16),
        jnp.zeros(pre_shape, jnp.float32),
        jnp.zeros((micro, rows, width), jnp.bfloat16),
    )
    _, saved_in, saved_pre, outputs = lax.fori_loop(0, ticks, forward_tick, start)

    def backward_tick(t, carry):
        incoming, grads_in, slopes = carry
        step_m = t - (sections - 1 - section_idx)
        valid = (step_m >= 0) & (step_m < micro)
        index = jnp.clip(step_m, 0, micro - 1)
        d_now = jnp.where(section_idx == sections - 1, take_row(cotangent, index), incoming)

        def backward_active(state):
            keep_grads, keep_slopes = state
            xf, r, n = norm_parts(take_row(saved_in, index), g_local)
            a = take_row(saved_pre, index)
            d_f = d_now.astype(jnp.float32)
            slope = (d_f * silu_slope(a)).astype(jnp.bfloat16)
            e_back = lax.dot_general(
                slope, w_local, (((1,), (1,)), ((), ())), preferred_element_type=jnp.float32
            )
            h_back = g_local * e_back
            dx = d_f + r * h_back - xf * r**3 * jnp.mean(xf * h_back, -1, keepdims=True)
            d_out = dx.astype(jnp.bfloat16)
            return (d_out, (put_row(keep_grads, d_out, index), put_row(keep_slopes, slope, index)))

        def backward_passive(state):
            return (zero_rows, state)

        d_out, state = lax.cond(valid, backward_active, backward_passive, (grads_in, slopes))
        sent = passed_along(d_out, "section", -1)
        return (sent,) + state

    start_back = (
        zero_rows,
        jnp.zeros((micro, rows, width), jnp.bfloat16),
        jnp.zeros((micro, rows, width), jnp.bfloat16),
    )
    _, grads_in, slopes = lax.fori_loop(0, ticks, backward_tick, start_back)
    _, _, normed = norm_parts(saved_in, g_local)
    local_grad = lax.dot_general(
        normed.reshape(-1, width),
        slopes.reshape(-1, width),
        (((0,), (0,)), ((), ())),
        preferred_element_type=jnp.float32,
    )
    groups = lax.axis_size("dp")
    grad_scale = (micro * rows * groups) ** (-0.5)
    share = width // groups
    total = lax.psum(local_grad.astype(jnp.bfloat16), "dp").astype(jnp.float32)
    mine = lax.dynamic_slice_in_dim(total, lax.axis_index("dp") * share, share, 0)
    return (outputs[None], grads_in[None], (mine * grad_scale)[None])


def solution(mesh):
    in_specs = (
        P(None, "dp", None),
        P(None, "dp", None),
        P("section", None, None),
        P("section", None),
    )
    out_specs = (
        P("section", None, "dp", None),
        P("section", None, "dp", None),
        P("section", "dp", None),
    )
    return jax.shard_map(body, mesh=mesh, in_specs=in_specs, out_specs=out_specs, check_vma=False)
```

profile of v0, /device:TPU:1, one launch (start us, length us, event | category | flops | bytes accessed | tf_op | source)
XLA Modules:
  0.0 783.5 jit_solution(9882055556957927038)
XLA Ops:
  10.0 176.3 %while.39 = (s32[]{:T(128)}, bf16[64,2560]{1,0:T(8,128)(2,1)S(1)}, bf16[4,64,2560]{2,1,0:T(8,128)(2,1)S(1)}, f32[4,64,2560]{2,1,0:T(8,128)}, bf16[4,64,2560]{2,1...) while((s32[]{:T(128)}, bf16[64,2560]{1,0:T(8,128)(2,1)S(1)}, ...), condition=%wide.region_4.5_spmd, body=%wide.region_0.4_spmd.sunk | while | flops 841318464 | bytes 19367540 | solution.py:73
  10.0 9.4 %conditional.4 = (bf16[64,2560]{1,0:T(8,128)(2,1)S(1)}, bf16[4,64,2560]{2,1,0:T(8,128)(2,1)S(1)}, f32[4,64,2560]{2,1,0:T(8,128)}, bf16[4,64,2560]{2,1,0:T(8,128)(2,1)S(1)}) conditional(s32[]{:T(128)} %convert_element_type.129, (bf16[4,64,2560]{2,1,0:T(8,128)(2,1)S(1)}, f32[4,64,2560]{2,1,0:T(8,128)}, bf16[4,64,2560]{2,1,0:T(8,128)(2,1)S(1)}) %tuple.111, ...), branch_computations={%region_1.1_spmd, %region_2.3_spmd} | conditional | flops 841318464 | bytes 18056520 | solution.py:63
  11.3 7.2 bitcast_dynamic-update-slice_fusion.1
  20.7 5.8 collective-permute-done
  26.5 9.4 %conditional.4 = (bf16[64,2560]{1,0:T(8,128)(2,1)S(1)}, bf16[4,64,2560]{2,1,0:T(8,128)(2,1)S(1)}, f32[4,64,2560]{2,1,0:T(8,128)}, bf16[4,64,2560]{2,1,0:T(8,128)(2,1)S(1)}) conditional(s32[]{:T(128)} %convert_element_type.129, (bf16[4,64,2560]{2,1,0:T(8,128)(2,1)S(1)}, f32[4,64,2560]{2,1,0:T(8,128)}, bf16[4,64,2560]{2,1,0:T(8,128)(2,1)S(1)}) %tuple.111, ...), branch_computations={%region_1.1_spmd, %region_2.3_spmd} | conditional | flops 841318464 | bytes 18056520 | solution.py:63
  27.8 7.2 bitcast_dynamic-update-slice_fusion.1
  36.0 5.6 collective-permute-start
  41.6 4.9 collective-permute-done
  46.5 9.4 %conditional.4 = (bf16[64,2560]{1,0:T(8,128)(2,1)S(1)}, bf16[4,64,2560]{2,1,0:T(8,128)(2,1)S(1)}, f32[4,64,2560]{2,1,0:T(8,128)}, bf16[4,64,2560]{2,1,0:T(8,128)(2,1)S(1)}) conditional(s32[]{:T(128)} %convert_element_type.129, (bf16[4,64,2560]{2,1,0:T(8,128)(2,1)S(1)}, f32[4,64,2560]{2,1,0:T(8,128)}, bf16[4,64,2560]{2,1,0:T(8,128)(2,1)S(1)}) %tuple.111, ...), branch_computations={%region_1.1_spmd, %region_2.3_spmd} | conditional | flops 841318464 | bytes 18056520 | solution.py:63
  47.7 7.2 bitcast_dynamic-update-slice_fusion.1
  55.9 5.6 collective-permute-start
  61.5 4.0 collective-permute-done
  65.5 9.4 %conditional.4 = (bf16[64,2560]{1,0:T(8,128)(2,1)S(1)}, bf16[4,64,2560]{2,1,0:T(8,128)(2,1)S(1)}, f32[4,64,2560]{2,1,0:T(8,128)}, bf16[4,64,2560]{2,1,0:T(8,128)(2,1)S(1)}) conditional(s32[]{:T(128)} %convert_element_type.129, (bf16[4,64,2560]{2,1,0:T(8,128)(2,1)S(1)}, f32[4,64,2560]{2,1,0:T(8,128)}, bf16[4,64,2560]{2,1,0:T(8,128)(2,1)S(1)}) %tuple.111, ...), branch_computations={%region_1.1_spmd, %region_2.3_spmd} | conditional | flops 841318464 | bytes 18056520 | solution.py:63
  66.8 7.2 bitcast_dynamic-update-slice_fusion.1
  74.9 5.3 collective-permute-start
  80.3 4.0 collective-permute-done
  84.3 14.7 %collective-permute-start = (bf16[64,2560]{1,0:T(8,128)(2,1)S(1)}, bf16[64,2560]{1,0:T(8,128)(2,1)S(1)}, u32[]{:S(2)}, u32[]{:S(2)}) collective-permute-start(bf16[64,2560]{1,0:T(8,128)(2,1)S(1)} %get-tuple-element.865), channel_id=1, source_target_pairs={{0,16},{16,32},{32,48},{48,64},{64,80},{80,96},{96,112},{1,17},{17... | collective-permute-start | bytes 983048 | tf_op jit(solution)/shard_map/while/body/eval_jaxpr/ppermute | solution.py:12
  103.0 5.5 collective-permute-start
  112.5 15.6 %collective-permute-start = (bf16[64,2560]{1,0:T(8,128)(2,1)S(1)}, bf16[64,2560]{1,0:T(8,128)(2,1)S(1)}, u32[]{:S(2)}, u32[]{:S(2)}) collective-permute-start(bf16[64,2560]{1,0:T(8,128)(2,1)S(1)} %get-tuple-element.865), channel_id=1, source_target_pairs={{0,16},{16,32},{32,48},{48,64},{64,80},{80,96},{96,112},{1,17},{17... | collective-permute-start | bytes 983048 | tf_op jit(solution)/shard_map/while/body/eval_jaxpr/ppermute | solution.py:12
  132.1 6.2 collective-permute-start
  138.4 4.5 collective-permute-done
  142.9 9.9 %collective-permute-start = (bf16[64,2560]{1,0:T(8,128)(2,1)S(1)}, bf16[64,2560]{1,0:T(8,128)(2,1)S(1)}, u32[]{:S(2)}, u32[]{:S(2)}) collective-permute-start(bf16[64,2560]{1,0:T(8,128)(2,1)S(1)} %get-tuple-element.865), channel_id=1, source_target_pairs={{0,16},{16,32},{32,48},{48,64},{64,80},{80,96},{96,112},{1,17},{17... | collective-permute-start | bytes 983048 | tf_op jit(solution)/shard_map/while/body/eval_jaxpr/ppermute | solution.py:12
  156.8 8.9 %collective-permute-start = (bf16[64,2560]{1,0:T(8,128)(2,1)S(1)}, bf16[64,2560]{1,0:T(8,128)(2,1)S(1)}, u32[]{:S(2)}, u32[]{:S(2)}) collective-permute-start(bf16[64,2560]{1,0:T(8,128)(2,1)S(1)} %get-tuple-element.865), channel_id=1, source_target_pairs={{0,16},{16,32},{32,48},{48,64},{64,80},{80,96},{96,112},{1,17},{17... | collective-permute-start | bytes 983048 | tf_op jit(solution)/shard_map/while/body/eval_jaxpr/ppermute | solution.py:12
  165.8 7.0 collective-permute-done
  172.8 6.5 collective-permute-start
  179.3 7.0 collective-permute-done
  189.7 260.8 %while.40 = (s32[]{:T(128)}, bf16[64,2560]{1,0:T(8,128)(2,1)S(1)}, bf16[4,64,2560]{2,1,0:T(8,128)(2,1)}, bf16[4,64,2560]{2,1,0:T(8,128)(2,1)}, s32[]{:T(128)}, /...) while((s32[]{:T(128)}, bf16[64,2560]{1,0:T(8,128)(2,1)S(1)}, ...), condition=%wide.region_10.11_spmd, body=%wide.region_5.10_spmd.sunk | while | flops 843120832 | bytes 20023156 | solution.py:108
  191.1 14.1 %collective-permute-done.1 = bf16[64,2560]{1,0:T(8,128)(2,1)S(1)} collective-permute-done((bf16[64,2560]{1,0:T(8,128)(2,1)S(1)}, bf16[64,2560]{1,0:T(8,128)(2,1)S(1)}, u32[]{:S(2)}, u32[]{:S(2)}) %collective-permute-start.1) | collective-permute-done | bytes 327712 | tf_op jit(solution)/shard_map/while/body/eval_jaxpr/ppermute | solution.py:12
  206.5 9.5 %collective-permute-done.1 = bf16[64,2560]{1,0:T(8,128)(2,1)S(1)} collective-permute-done((bf16[64,2560]{1,0:T(8,128)(2,1)S(1)}, bf16[64,2560]{1,0:T(8,128)(2,1)S(1)}, u32[]{:S(2)}, u32[]{:S(2)}) %collective-permute-start.1) | collective-permute-done | bytes 327712 | tf_op jit(solution)/shard_map/while/body/eval_jaxpr/ppermute | solution.py:12
  217.4 17.3 %collective-permute-done.1 = bf16[64,2560]{1,0:T(8,128)(2,1)S(1)} collective-permute-done((bf16[64,2560]{1,0:T(8,128)(2,1)S(1)}, bf16[64,2560]{1,0:T(8,128)(2,1)S(1)}, u32[]{:S(2)}, u32[]{:S(2)}) %collective-permute-start.1) | collective-permute-done | bytes 327712 | tf_op jit(solution)/shard_map/while/body/eval_jaxpr/ppermute | solution.py:12
  236.0 10.4 %collective-permute-done.1 = bf16[64,2560]{1,0:T(8,128)(2,1)S(1)} collective-permute-done((bf16[64,2560]{1,0:T(8,128)(2,1)S(1)}, bf16[64,2560]{1,0:T(8,128)(2,1)S(1)}, u32[]{:S(2)}, u32[]{:S(2)}) %collective-permute-start.1) | collective-permute-done | bytes 327712 | tf_op jit(solution)/shard_map/while/body/eval_jaxpr/ppermute | solution.py:12
  247.8 17.9 %collective-permute-done.1 = bf16[64,2560]{1,0:T(8,128)(2,1)S(1)} collective-permute-done((bf16[64,2560]{1,0:T(8,128)(2,1)S(1)}, bf16[64,2560]{1,0:T(8,128)(2,1)S(1)}, u32[]{:S(2)}, u32[]{:S(2)}) %collective-permute-start.1) | collective-permute-done | bytes 327712 | tf_op jit(solution)/shard_map/while/body/eval_jaxpr/ppermute | solution.py:12
  267.0 11.5 %collective-permute-done.1 = bf16[64,2560]{1,0:T(8,128)(2,1)S(1)} collective-permute-done((bf16[64,2560]{1,0:T(8,128)(2,1)S(1)}, bf16[64,2560]{1,0:T(8,128)(2,1)S(1)}, u32[]{:S(2)}, u32[]{:S(2)}) %collective-permute-start.1) | collective-permute-done | bytes 327712 | tf_op jit(solution)/shard_map/while/body/eval_jaxpr/ppermute | solution.py:12
  279.9 76.9 %collective-permute-done.1 = bf16[64,2560]{1,0:T(8,128)(2,1)S(1)} collective-permute-done((bf16[64,2560]{1,0:T(8,128)(2,1)S(1)}, bf16[64,2560]{1,0:T(8,128)(2,1)S(1)}, u32[]{:S(2)}, u32[]{:S(2)}) %collective-permute-start.1) | collective-permute-done | bytes 327712 | tf_op jit(solution)/shard_map/while/body/eval_jaxpr/ppermute | solution.py:12
  356.8 12.0 %conditional.5 = (bf16[64,2560]{1,0:T(8,128)(2,1)S(1)}, bf16[4,64,2560]{2,1,0:T(8,128)(2,1)}, bf16[4,64,2560]{2,1,0:T(8,128)(2,1)}) conditional(s32[]{:T(128)} %convert_element_type.130, (bf16[4,64,2560]{2,1,0:T(8,128)(2,1)}, bf16[4,64,2560]{2,1,0:T(8,128)(2,1)}) %tuple.114, (pred[]{:T(512)}, s32[]{:T(128)}, bf16[4,64,2560]{2,1,0:T(8,128)(2,1)S(1)}, ...), branch_computations={%region_6.6_spmd, %region_7.9_spmd} | conditional | flops 843120832 | bytes 18712128 | solution.py:99
  358.9 8.9 %fusion.11 = (f32[64]{0:T(128)S(1)}, f32[64]{0:T(128)S(1)}, f32[64,2560]{1,0:T(8,128)S(1)}) fusion(bf16[4,64,2560]{2,1,0:T(8,128)(2,1)S(1)} %get-tuple-element.650, s32[]{:T(128)S(6)} %min.21, bf16[64,2560]{1,0:T(8,128)(2,1)S(1)} %get-tuple-element.733, bf16[2560,2560]{1,0:T(8,128)(2,1)} %get-tuple-element.653, f32[2560]{0:T(1024)S(1)} %reduce.1), kind=kOutput, calls=%fused_computation.24 | convolution fusion | flops 839843712 | bytes 14428676 | tf_op jit(solution)/shard_map/while/body/eval_jaxpr/cond/branch_1_fun/dot_general | solution.py:88
  370.1 9.2 %collective-permute-done.1 = bf16[64,2560]{1,0:T(8,128)(2,1)S(1)} collective-permute-done((bf16[64,2560]{1,0:T(8,128)(2,1)S(1)}, bf16[64,2560]{1,0:T(8,128)(2,1)S(1)}, u32[]{:S(2)}, u32[]{:S(2)}) %collective-permute-start.1) | collective-permute-done | bytes 327712 | tf_op jit(solution)/shard_map/while/body/eval_jaxpr/ppermute | solution.py:12
  379.2 12.0 %conditional.5 = (bf16[64,2560]{1,0:T(8,128)(2,1)S(1)}, bf16[4,64,2560]{2,1,0:T(8,128)(2,1)}, bf16[4,64,2560]{2,1,0:T(8,128)(2,1)}) conditional(s32[]{:T(128)} %convert_element_type.130, (bf16[4,64,2560]{2,1,0:T(8,128)(2,1)}, bf16[4,64,2560]{2,1,0:T(8,128)(2,1)}) %tuple.114, (pred[]{:T(512)}, s32[]{:T(128)}, bf16[4,64,2560]{2,1,0:T(8,128)(2,1)S(1)}, ...), branch_computations={%region_6.6_spmd, %region_7.9_spmd} | conditional | flops 843120832 | bytes 18712128 | solution.py:99
  381.4 8.9 %fusion.11 = (f32[64]{0:T(128)S(1)}, f32[64]{0:T(128)S(1)}, f32[64,2560]{1,0:T(8,128)S(1)}) fusion(bf16[4,64,2560]{2,1,0:T(8,128)(2,1)S(1)} %get-tuple-element.650, s32[]{:T(128)S(6)} %min.21, bf16[64,2560]{1,0:T(8,128)(2,1)S(1)} %get-tuple-element.733, bf16[2560,2560]{1,0:T(8,128)(2,1)} %get-tuple-element.653, f32[2560]{0:T(1024)S(1)} %reduce.1), kind=kOutput, calls=%fused_computation.24 | convolution fusion | flops 839843712 | bytes 14428676 | tf_op jit(solution)/shard_map/while/body/eval_jaxpr/cond/branch_1_fun/dot_general | solution.py:88
  392.6 10.5 %collective-permute-done.1 = bf16[64,2560]{1,0:T(8,128)(2,1)S(1)} collective-permute-done((bf16[64,2560]{1,0:T(8,128)(2,1)S(1)}, bf16[64,2560]{1,0:T(8,128)(2,1)S(1)}, u32[]{:S(2)}, u32[]{:S(2)}) %collective-permute-start.1) | collective-permute-done | bytes 327712 | tf_op jit(solution)/shard_map/while/body/eval_jaxpr/ppermute | solution.py:12
  403.1 12.0 %conditional.5 = (bf16[64,2560]{1,0:T(8,128)(2,1)S(1)}, bf16[4,64,2560]{2,1,0:T(8,128)(2,1)}, bf16[4,64,2560]{2,1,0:T(8,128)(2,1)}) conditional(s32[]{:T(128)} %convert_element_type.130, (bf16[4,64,2560]{2,1,0:T(8,128)(2,1)}, bf16[4,64,2560]{2,1,0:T(8,128)(2,1)}) %tuple.114, (pred[]{:T(512)}, s32[]{:T(128)}, bf16[4,64,2560]{2,1,0:T(8,128)(2,1)S(1)}, ...), branch_computations={%region_6.6_spmd, %region_7.9_spmd} | conditional | flops 843120832 | bytes 18712128 | solution.py:99
  405.2 8.9 %fusion.11 = (f32[64]{0:T(128)S(1)}, f32[64]{0:T(128)S(1)}, f32[64,2560]{1,0:T(8,128)S(1)}) fusion(bf16[4,64,2560]{2,1,0:T(8,128)(2,1)S(1)} %get-tuple-element.650, s32[]{:T(128)S(6)} %min.21, bf16[64,2560]{1,0:T(8,128)(2,1)S(1)} %get-tuple-element.733, bf16[2560,2560]{1,0:T(8,128)(2,1)} %get-tuple-element.653, f32[2560]{0:T(1024)S(1)} %reduce.1), kind=kOutput, calls=%fused_computation.24 | convolution fusion | flops 839843712 | bytes 14428676 | tf_op jit(solution)/shard_map/while/body/eval_jaxpr/cond/branch_1_fun/dot_general | solution.py:88
  416.4 11.9 %collective-permute-done.1 = bf16[64,2560]{1,0:T(8,128)(2,1)S(1)} collective-permute-done((bf16[64,2560]{1,0:T(8,128)(2,1)S(1)}, bf16[64,2560]{1,0:T(8,128)(2,1)S(1)}, u32[]{:S(2)}, u32[]{:S(2)}) %collective-permute-start.1) | collective-permute-done | bytes 327712 | tf_op jit(solution)/shard_map/while/body/eval_jaxpr/ppermute | solution.py:12
  428.3 12.0 %conditional.5 = (bf16[64,2560]{1,0:T(8,128)(2,1)S(1)}, bf16[4,64,2560]{2,1,0:T(8,128)(2,1)}, bf16[4,64,2560]{2,1,0:T(8,128)(2,1)}) conditional(s32[]{:T(128)} %convert_element_type.130, (bf16[4,64,2560]{2,1,0:T(8,128)(2,1)}, bf16[4,64,2560]{2,1,0:T(8,128)(2,1)}) %tuple.114, (pred[]{:T(512)}, s32[]{:T(128)}, bf16[4,64,2560]{2,1,0:T(8,128)(2,1)S(1)}, ...), branch_computations={%region_6.6_spmd, %region_7.9_spmd} | conditional | flops 843120832 | bytes 18712128 | solution.py:99
  430.4 8.9 %fusion.11 = (f32[64]{0:T(128)S(1)}, f32[64]{0:T(128)S(1)}, f32[64,2560]{1,0:T(8,128)S(1)}) fusion(bf16[4,64,2560]{2,1,0:T(8,128)(2,1)S(1)} %get-tuple-element.650, s32[]{:T(128)S(6)} %min.21, bf16[64,2560]{1,0:T(8,128)(2,1)S(1)} %get-tuple-element.733, bf16[2560,2560]{1,0:T(8,128)(2,1)} %get-tuple-element.653, f32[2560]{0:T(1024)S(1)} %reduce.1), kind=kOutput, calls=%fused_computation.24 | convolution fusion | flops 839843712 | bytes 14428676 | tf_op jit(solution)/shard_map/while/body/eval_jaxpr/cond/branch_1_fun/dot_general | solution.py:88
  441.6 8.9 %collective-permute-done.1 = bf16[64,2560]{1,0:T(8,128)(2,1)S(1)} collective-permute-done((bf16[64,2560]{1,0:T(8,128)(2,1)S(1)}, bf16[64,2560]{1,0:T(8,128)(2,1)S(1)}, u32[]{:S(2)}, u32[]{:S(2)}) %collective-permute-start.1) | collective-permute-done | bytes 327712 | tf_op jit(solution)/shard_map/while/body/eval_jaxpr/ppermute | solution.py:12
  450.5 8.1 %bitcast_convert_fusion = bf16[2560,2560]{1,0:T(8,128)(2,1)} fusion(bf16[4,64,2560]{2,1,0:T(8,128)(2,1)} %get-tuple-element.683, bf16[4,64,2560]{2,1,0:T(8,128)(2,1)S(1)} %get-tuple-element.981, f32[2560]{0:T(1024)S(1)} %reduce.2, f32[4,64]{1,0:T(4,128)S(1)} %add_rsqrt_fusion.2), kind=kOutput, calls=%fused_computation.40 | convolution fusion | flops 3364618240 | bytes 15739904 | tf_op jit(solution)/shard_map/dot_general | solution.py:110
  458.6 315.6 %all-reduce.2.cloned.1.call-done = bf16[2560,2560]{1,0:T(8,128)(2,1)} async-done(((bf16[2560,2560]{1,0:T(8,128)(2,1)}), bf16[2560,2560]{1,0:T(8,128)(2,1)}) %all-reduce.2.cloned.1.call-update) | async-done | bytes 13107216 | tf_op jit(solution)/shard_map/psum | solution.py:119
  (99 shorter events, 62.1 us)
Async XLA Ops:
  7.2 767.0 %all-reduce.2.cloned.1.call-start = ((), (), s32[]{:S(2)}) async-start(), calls=%async_computation | async-start | bytes 26214400 | tf_op jit(solution)/shard_map/psum | solution.py:119
  8.2 1.8 copy-start.2
  19.4 7.1 collective-permute-start
  36.0 10.5 %collective-permute-start = (bf16[64,2560]{1,0:T(8,128)(2,1)S(1)}, bf16[64,2560]{1,0:T(8,128)(2,1)S(1)}, u32[]{:S(2)}, u32[]{:S(2)}) collective-permute-start(bf16[64,2560]{1,0:T(8,128)(2,1)S(1)} %get-tuple-element.865), channel_id=1, source_target_pairs={{0,16},{16,32},{32,48},{48,64},{64,80},{80,96},{96,112},{1,17},{17... | collective-permute-start | bytes 983048 | tf_op jit(solution)/shard_map/while/body/eval_jaxpr/ppermute | solution.py:12
  55.9 9.6 %collective-permute-start = (bf16[64,2560]{1,0:T(8,128)(2,1)S(1)}, bf16[64,2560]{1,0:T(8,128)(2,1)S(1)}, u32[]{:S(2)}, u32[]{:S(2)}) collective-permute-start(bf16[64,2560]{1,0:T(8,128)(2,1)S(1)} %get-tuple-element.865), channel_id=1, source_target_pairs={{0,16},{16,32},{32,48},{48,64},{64,80},{80,96},{96,112},{1,17},{17... | collective-permute-start | bytes 983048 | tf_op jit(solution)/shard_map/while/body/eval_jaxpr/ppermute | solution.py:12
  74.9 9.3 %collective-permute-start = (bf16[64,2560]{1,0:T(8,128)(2,1)S(1)}, bf16[64,2560]{1,0:T(8,128)(2,1)S(1)}, u32[]{:S(2)}, u32[]{:S(2)}) collective-permute-start(bf16[64,2560]{1,0:T(8,128)(2,1)S(1)} %get-tuple-element.865), channel_id=1, source_target_pairs={{0,16},{16,32},{32,48},{48,64},{64,80},{80,96},{96,112},{1,17},{17... | collective-permute-start | bytes 983048 | tf_op jit(solution)/shard_map/while/body/eval_jaxpr/ppermute | solution.py:12
  84.3 18.7 %collective-permute-start = (bf16[64,2560]{1,0:T(8,128)(2,1)S(1)}, bf16[64,2560]{1,0:T(8,128)(2,1)S(1)}, u32[]{:S(2)}, u32[]{:S(2)}) collective-permute-start(bf16[64,2560]{1,0:T(8,128)(2,1)S(1)} %get-tuple-element.865), channel_id=1, source_target_pairs={{0,16},{16,32},{32,48},{48,64},{64,80},{80,96},{96,112},{1,17},{17... | collective-permute-start | bytes 983048 | tf_op jit(solution)/shard_map/while/body/eval_jaxpr/ppermute | solution.py:12
  103.0 9.4 %collective-permute-start = (bf16[64,2560]{1,0:T(8,128)(2,1)S(1)}, bf16[64,2560]{1,0:T(8,128)(2,1)S(1)}, u32[]{:S(2)}, u32[]{:S(2)}) collective-permute-start(bf16[64,2560]{1,0:T(8,128)(2,1)S(1)} %get-tuple-element.865), channel_id=1, source_target_pairs={{0,16},{16,32},{32,48},{48,64},{64,80},{80,96},{96,112},{1,17},{17... | collective-permute-start | bytes 983048 | tf_op jit(solution)/shard_map/while/body/eval_jaxpr/ppermute | solution.py:12
  112.5 19.6 %collective-permute-start = (bf16[64,2560]{1,0:T(8,128)(2,1)S(1)}, bf16[64,2560]{1,0:T(8,128)(2,1)S(1)}, u32[]{:S(2)}, u32[]{:S(2)}) collective-permute-start(bf16[64,2560]{1,0:T(8,128)(2,1)S(1)} %get-tuple-element.865), channel_id=1, source_target_pairs={{0,16},{16,32},{32,48},{48,64},{64,80},{80,96},{96,112},{1,17},{17... | collective-permute-start | bytes 983048 | tf_op jit(solution)/shard_map/while/body/eval_jaxpr/ppermute | solution.py:12
  132.1 10.7 %collective-permute-start = (bf16[64,2560]{1,0:T(8,128)(2,1)S(1)}, bf16[64,2560]{1,0:T(8,128)(2,1)S(1)}, u32[]{:S(2)}, u32[]{:S(2)}) collective-permute-start(bf16[64,2560]{1,0:T(8,128)(2,1)S(1)} %get-tuple-element.865), channel_id=1, source_target_pairs={{0,16},{16,32},{32,48},{48,64},{64,80},{80,96},{96,112},{1,17},{17... | collective-permute-start | bytes 983048 | tf_op jit(solution)/shard_map/while/body/eval_jaxpr/ppermute | solution.py:12
  142.9 13.9 %collective-permute-start = (bf16[64,2560]{1,0:T(8,128)(2,1)S(1)}, bf16[64,2560]{1,0:T(8,128)(2,1)S(1)}, u32[]{:S(2)}, u32[]{:S(2)}) collective-permute-start(bf16[64,2560]{1,0:T(8,128)(2,1)S(1)} %get-tuple-element.865), channel_id=1, source_target_pairs={{0,16},{16,32},{32,48},{48,64},{64,80},{80,96},{96,112},{1,17},{17... | collective-permute-start | bytes 983048 | tf_op jit(solution)/shard_map/while/body/eval_jaxpr/ppermute | solution.py:12
  156.8 15.9 %collective-permute-start = (bf16[64,2560]{1,0:T(8,128)(2,1)S(1)}, bf16[64,2560]{1,0:T(8,128)(2,1)S(1)}, u32[]{:S(2)}, u32[]{:S(2)}) collective-permute-start(bf16[64,2560]{1,0:T(8,128)(2,1)S(1)} %get-tuple-element.865), channel_id=1, source_target_pairs={{0,16},{16,32},{32,48},{48,64},{64,80},{80,96},{96,112},{1,17},{17... | collective-permute-start | bytes 983048 | tf_op jit(solution)/shard_map/while/body/eval_jaxpr/ppermute | solution.py:12
  172.8 13.5 %collective-permute-start = (bf16[64,2560]{1,0:T(8,128)(2,1)S(1)}, bf16[64,2560]{1,0:T(8,128)(2,1)S(1)}, u32[]{:S(2)}, u32[]{:S(2)}) collective-permute-start(bf16[64,2560]{1,0:T(8,128)(2,1)S(1)} %get-tuple-element.865), channel_id=1, source_target_pairs={{0,16},{16,32},{32,48},{48,64},{64,80},{80,96},{96,112},{1,17},{17... | collective-permute-start | bytes 983048 | tf_op jit(solution)/shard_map/while/body/eval_jaxpr/ppermute | solution.py:12
  186.3 1.1 copy-start.1
  187.4 2.3 copy-start
  189.8 15.4 %collective-permute-start.1 = (bf16[64,2560]{1,0:T(8,128)(2,1)S(1)}, bf16[64,2560]{1,0:T(8,128)(2,1)S(1)}, u32[]{:S(2)}, u32[]{:S(2)}) collective-permute-start(bf16[64,2560]{1,0:T(8,128)(2,1)S(1)} %get-tuple-element.880), channel_id=1, source_target_pairs={{16,0},{32,16},{48,32},{64,48},{80,64},{96,80},{112,96},{17,1},{33... | collective-permute-start | bytes 983048 | tf_op jit(solution)/shard_map/while/body/eval_jaxpr/ppermute | solution.py:12
  205.2 10.9 %collective-permute-start.1 = (bf16[64,2560]{1,0:T(8,128)(2,1)S(1)}, bf16[64,2560]{1,0:T(8,128)(2,1)S(1)}, u32[]{:S(2)}, u32[]{:S(2)}) collective-permute-start(bf16[64,2560]{1,0:T(8,128)(2,1)S(1)} %get-tuple-element.880), channel_id=1, source_target_pairs={{16,0},{32,16},{48,32},{64,48},{80,64},{96,80},{112,96},{17,1},{33... | collective-permute-start | bytes 983048 | tf_op jit(solution)/shard_map/while/body/eval_jaxpr/ppermute | solution.py:12
  216.1 18.6 %collective-permute-start.1 = (bf16[64,2560]{1,0:T(8,128)(2,1)S(1)}, bf16[64,2560]{1,0:T(8,128)(2,1)S(1)}, u32[]{:S(2)}, u32[]{:S(2)}) collective-permute-start(bf16[64,2560]{1,0:T(8,128)(2,1)S(1)} %get-tuple-element.880), channel_id=1, source_target_pairs={{16,0},{32,16},{48,32},{64,48},{80,64},{96,80},{112,96},{17,1},{33... | collective-permute-start | bytes 983048 | tf_op jit(solution)/shard_map/while/body/eval_jaxpr/ppermute | solution.py:12
  234.7 11.7 %collective-permute-start.1 = (bf16[64,2560]{1,0:T(8,128)(2,1)S(1)}, bf16[64,2560]{1,0:T(8,128)(2,1)S(1)}, u32[]{:S(2)}, u32[]{:S(2)}) collective-permute-start(bf16[64,2560]{1,0:T(8,128)(2,1)S(1)} %get-tuple-element.880), channel_id=1, source_target_pairs={{16,0},{32,16},{48,32},{64,48},{80,64},{96,80},{112,96},{17,1},{33... | collective-permute-start | bytes 983048 | tf_op jit(solution)/shard_map/while/body/eval_jaxpr/ppermute | solution.py:12
  246.5 19.2 %collective-permute-start.1 = (bf16[64,2560]{1,0:T(8,128)(2,1)S(1)}, bf16[64,2560]{1,0:T(8,128)(2,1)S(1)}, u32[]{:S(2)}, u32[]{:S(2)}) collective-permute-start(bf16[64,2560]{1,0:T(8,128)(2,1)S(1)} %get-tuple-element.880), channel_id=1, source_target_pairs={{16,0},{32,16},{48,32},{64,48},{80,64},{96,80},{112,96},{17,1},{33... | collective-permute-start | bytes 983048 | tf_op jit(solution)/shard_map/while/body/eval_jaxpr/ppermute | solution.py:12
  265.7 12.8 %collective-permute-start.1 = (bf16[64,2560]{1,0:T(8,128)(2,1)S(1)}, bf16[64,2560]{1,0:T(8,128)(2,1)S(1)}, u32[]{:S(2)}, u32[]{:S(2)}) collective-permute-start(bf16[64,2560]{1,0:T(8,128)(2,1)S(1)} %get-tuple-element.880), channel_id=1, source_target_pairs={{16,0},{32,16},{48,32},{64,48},{80,64},{96,80},{112,96},{17,1},{33... | collective-permute-start | bytes 983048 | tf_op jit(solution)/shard_map/while/body/eval_jaxpr/ppermute | solution.py:12
  278.6 78.2 %collective-permute-start.1 = (bf16[64,2560]{1,0:T(8,128)(2,1)S(1)}, bf16[64,2560]{1,0:T(8,128)(2,1)S(1)}, u32[]{:S(2)}, u32[]{:S(2)}) collective-permute-start(bf16[64,2560]{1,0:T(8,128)(2,1)S(1)} %get-tuple-element.880), channel_id=1, source_target_pairs={{16,0},{32,16},{48,32},{64,48},{80,64},{96,80},{112,96},{17,1},{33... | collective-permute-start | bytes 983048 | tf_op jit(solution)/shard_map/while/body/eval_jaxpr/ppermute | solution.py:12
  368.8 10.5 %collective-permute-start.1 = (bf16[64,2560]{1,0:T(8,128)(2,1)S(1)}, bf16[64,2560]{1,0:T(8,128)(2,1)S(1)}, u32[]{:S(2)}, u32[]{:S(2)}) collective-permute-start(bf16[64,2560]{1,0:T(8,128)(2,1)S(1)} %get-tuple-element.880), channel_id=1, source_target_pairs={{16,0},{32,16},{48,32},{64,48},{80,64},{96,80},{112,96},{17,1},{33... | collective-permute-start | bytes 983048 | tf_op jit(solution)/shard_map/while/body/eval_jaxpr/ppermute | solution.py:12
  391.3 11.8 %collective-permute-start.1 = (bf16[64,2560]{1,0:T(8,128)(2,1)S(1)}, bf16[64,2560]{1,0:T(8,128)(2,1)S(1)}, u32[]{:S(2)}, u32[]{:S(2)}) collective-permute-start(bf16[64,2560]{1,0:T(8,128)(2,1)S(1)} %get-tuple-element.880), channel_id=1, source_target_pairs={{16,0},{32,16},{48,32},{64,48},{80,64},{96,80},{112,96},{17,1},{33... | collective-permute-start | bytes 983048 | tf_op jit(solution)/shard_map/while/body/eval_jaxpr/ppermute | solution.py:12
  415.1 13.2 %collective-permute-start.1 = (bf16[64,2560]{1,0:T(8,128)(2,1)S(1)}, bf16[64,2560]{1,0:T(8,128)(2,1)S(1)}, u32[]{:S(2)}, u32[]{:S(2)}) collective-permute-start(bf16[64,2560]{1,0:T(8,128)(2,1)S(1)} %get-tuple-element.880), channel_id=1, source_target_pairs={{16,0},{32,16},{48,32},{64,48},{80,64},{96,80},{112,96},{17,1},{33... | collective-permute-start | bytes 983048 | tf_op jit(solution)/shard_map/while/body/eval_jaxpr/ppermute | solution.py:12
  440.3 10.2 %collective-permute-start.1 = (bf16[64,2560]{1,0:T(8,128)(2,1)S(1)}, bf16[64,2560]{1,0:T(8,128)(2,1)S(1)}, u32[]{:S(2)}, u32[]{:S(2)}) collective-permute-start(bf16[64,2560]{1,0:T(8,128)(2,1)S(1)} %get-tuple-element.880), channel_id=1, source_target_pairs={{16,0},{32,16},{48,32},{64,48},{80,64},{96,80},{112,96},{17,1},{33... | collective-permute-start | bytes 983048 | tf_op jit(solution)/shard_map/while/body/eval_jaxpr/ppermute | solution.py:12
Sparse Core Ops, SparseCore 0:
  458.7 315.3 all-reduce.1
where the time goes:
time: 785 us; the launch traced here: 783 us
  waiting for transfers between devices  567 us (72%)
  starting transfers between devices  99.4 us (13%)
  matrix products  72.5 us (9%)
  other arithmetic  21.2 us (3%)
  between operations  14.1 us (2%)
  local copies, waits for them, and re-layouts  9.03 us (1%)
    psum x1, waiting for transfers between devices, body(): total = lax.psum(local_grad.astype(jnp.bfloat16), 'dp').astype(jnp.float32)  316 us
    ppermute x22, waiting for transfers between devices, passed_along(): return lax.ppermute(array, axis, pairs)  251 us
    ppermute x22, starting transfers between devices, passed_along(): return lax.ppermute(array, axis, pairs)  99.3 us
    dot_general x4, matrix products, backward_active(): lax.dot_general(slope, w_local, (((1,), (1,)), ((), ())), preferred_eleme...  35.5 us
    dot_general x4, matrix products, forward_active(): a = jnp.dot(n, w_local, preferred_element_type=jnp.float32)  28.9 us
    dynamic_update_slice x12, other arithmetic, put_row(): return lax.dynamic_update_index_in_dim(buffer, value, index, 0)  16.6 us
  transfers between devices with their start and end apart: 23, of which 23 were waited for; matrix products, arithmetic and copies ran while one was open for 0% of the time, Pallas kernels for 0%

commit v1 on v0

v1 whole, which is shorter than its diff:
```python
import functools

import jax
import jax.numpy as jnp
from jax import lax
from jax.experimental import pallas as pl
from jax.experimental.pallas import tpu as pltpu
from jax.sharding import PartitionSpec as P

EPS = 1e-05
MESH = pl.DeviceIdType.MESH
BF16, F32 = jnp.bfloat16, jnp.float32

CHUNK = 64
PIECES = 5
SPLIT = 1408


def kernel(
    x_hbm, d_hbm, w_hbm, gain, acts, grads, wgrad,
    w_v, wt_v, xs, ds_in, slope, rinv, acc, n2, s2, nt, part, got_a1, got_a2, got_a3, got_b1, got_b2, got_b3,
    w_sem, f_send, f_recv, b_send, b_recv, n_send, n_recv, s_send, s_recv, r_send, r_recv,
):
    total, width = xs.shape
    count = total // CHUNK
    piece = width // PIECES
    share = wgrad.shape[0]
    section, dp = lax.axis_index("section"), lax.axis_index("dp")
    sections = lax.axis_size("section")
    x, y, core = dp // 4, (dp // 2) % 2, dp % 2
    first, last = section == 0, section == sections - 1

    def at(x_to, y_to, core_to):
        return (section, x_to * 4 + y_to * 2 + core_to)

    after, before = (section + 1, dp), (section - 1, dp)
    twin = at(x, y, 1 - core)
    right, left, across = at((x + 1) % 4, y, core), at((x + 3) % 4, y, core), at(x, 1 - y, core)

    def local(source, target, sem):
        return pltpu.make_async_copy(source, target, sem)

    def remote(source, target, send, recv, device):
        return pltpu.make_async_remote_copy(
            src_ref=source, dst_ref=target, send_sem=send, recv_sem=recv, device_id=device, device_id_type=MESH
        )

    def cols(p):
        return slice(p * piece, (p + 1) * piece)

    def rows_of(m):
        return pl.ds(pl.multiple_of(m * CHUNK, CHUNK), CHUNK)

    for p in range(PIECES):
        local(w_hbm.at[cols(p), :], w_v.at[cols(p), :], w_sem.at[p]).start()

    def fetch(source, target, sems):
        @pl.loop(0, count)
        def _(m):
            for p in range(PIECES):
                local(source.at[rows_of(m), cols(p)], target.at[rows_of(m), cols(p)], sems.at[m, p]).start()

    @pl.when(first)
    def _():
        fetch(x_hbm, xs, f_recv)

    @pl.when(last)
    def _():
        fetch(d_hbm, ds_in, b_recv)

    barrier = pltpu.get_barrier_semaphore()
    for device in (twin, right, left, across):
        pl.semaphore_signal(barrier, inc=1, device_id=device, device_id_type=MESH)

    @pl.when(section > 0)
    def _():
        pl.semaphore_signal(barrier, inc=1, device_id=before, device_id_type=MESH)

    @pl.when(section < sections - 1)
    def _():
        pl.semaphore_signal(barrier, inc=1, device_id=after, device_id_type=MESH)

    pl.semaphore_wait(barrier, 4 + (section > 0).astype(jnp.int32) + (section < sections - 1).astype(jnp.int32))

    def turn_weight():
        tile = 256

        @pl.loop(0, width // tile)
        def _(i):
            i = pl.ds(pl.multiple_of(i * tile, tile), tile)
            for j in range(0, width, tile):
                wt_v[j : j + tile, i] = w_v[i, j : j + tile].T

    def await_weight():
        for p in range(PIECES):
            local(w_hbm.at[cols(p), :], w_v.at[cols(p), :], w_sem.at[p]).wait()

    early = section >= sections // 2

    @pl.when(early)
    def _():
        await_weight()
        turn_weight()

    def add_product(lhs, rhs, p):
        tile = 512
        for j in range(0, width, tile):
            term = jnp.dot(lhs, rhs[cols(p), j : j + tile], preferred_element_type=F32)
            if p == 0:
                acc[:, j : j + tile] = term
            else:
                acc[:, j : j + tile] += term

    def lane_sum(values):
        out = values[:, :128]
        for j in range(128, values.shape[1], 128):
            out = out + values[:, j : j + 128]
        return out

    def forward(m, carry):
        rows = rows_of(m)
        squares = None
        for p in range(PIECES):
            local(xs.at[rows, cols(p)], xs.at[rows, cols(p)], f_recv.at[m, p]).wait()
            if p >= 0:

                @pl.when(jnp.logical_and(m == 0, jnp.logical_not(early)))
                def _():
                    local(w_hbm.at[cols(p), :], w_v.at[cols(p), :], w_sem.at[p]).wait()

            xf = xs[rows, cols(p)].astype(F32)
            term = lane_sum(xf * xf)
            squares = term if squares is None else squares + term
            add_product((xf * gain[:, cols(p)]).astype(BF16), w_v, p)
        r = lax.rsqrt(jnp.sum(squares, -1, keepdims=True) * (1.0 / width) + EPS)
        rinv[rows, :] = jnp.broadcast_to(r, (CHUNK, 128))
        for p in range(PIECES):
            a = acc[:, cols(p)] * r
            xf = xs[rows, cols(p)].astype(F32)
            sig = jax.nn.sigmoid(a)
            acts[rows, cols(p)] = (xf + a * sig).astype(BF16)

            @pl.when(section < sections - 1)
            def _():
                remote(
                    acts.at[rows, cols(p)], xs.at[rows, cols(p)], f_send.at[m, p], f_recv.at[m, p], after
                ).start()

            slope[rows, cols(p)] = sig * (1.0 + a * (1.0 - sig))
            n2[rows, cols(p)] = (xf * r * gain[:, cols(p)]).astype(BF16)
        remote(n2.at[rows, :], n2.at[pl.ds(pl.multiple_of(total + m * CHUNK, CHUNK), CHUNK), :], n_send.at[m], n_recv.at[m], twin).start()
        return carry

    lax.fori_loop(0, count, forward, 0)

    def turn_normed():
        tile = 256

        @pl.loop(0, count)
        def _(m):
            other = pl.ds(pl.multiple_of(total + m * CHUNK, CHUNK), CHUNK)
            remote(n2.at[rows_of(m), :], n2.at[other, :], n_send.at[m], n_recv.at[m], twin).wait_recv()

        @pl.loop(0, width // tile)
        def _(i):
            i = pl.ds(pl.multiple_of(i * tile, tile), tile)
            nt[i, :] = n2[:, i].T

    @pl.when(jnp.logical_not(early))
    def _():
        turn_weight()
        turn_normed()

    def backward(m, carry):
        rows = rows_of(m)
        for p in range(PIECES):
            local(ds_in.at[rows, cols(p)], ds_in.at[rows, cols(p)], b_recv.at[m, p]).wait()
            s = (ds_in[rows, cols(p)].astype(F32) * slope[rows, cols(p)]).astype(BF16)
            s2[rows, cols(p)] = s
            add_product(s, wt_v, p)
        remote(s2.at[rows, :], s2.at[pl.ds(pl.multiple_of(total + m * CHUNK, CHUNK), CHUNK), :], s_send.at[m], s_recv.at[m], twin).start()
        dots = None
        for p in range(PIECES):
            h = acc[:, cols(p)] * gain[:, cols(p)]
            acc[:, cols(p)] = h
            term = lane_sum(xs[rows, cols(p)].astype(F32) * h)
            dots = term if dots is None else dots + term
        r = rinv[rows, :1]
        scale = r * r * r * (jnp.sum(dots, -1, keepdims=True) * (1.0 / width))
        for p in range(PIECES):
            out = ds_in[rows, cols(p)].astype(F32) + r * acc[:, cols(p)] - xs[rows, cols(p)].astype(F32) * scale
            grads[rows, cols(p)] = out.astype(BF16)

            @pl.when(section > 0)
            def _():
                remote(
                    grads.at[rows, cols(p)], ds_in.at[rows, cols(p)], b_send.at[m, p], b_recv.at[m, p], before
                ).start()

        return carry

    lax.fori_loop(0, count, backward, 0)

    @pl.when(early)
    def _():
        turn_normed()

    @pl.loop(0, count)
    def _(m):
        other = pl.ds(pl.multiple_of(total + m * CHUNK, CHUNK), CHUNK)
        remote(s2.at[rows_of(m), :], s2.at[other, :], s_send.at[m], s_recv.at[m], twin).wait_recv()

    def block(x_to, y_to):
        return x_to * 2 + y_to

    def make_block(b):
        rows = pl.ds(pl.multiple_of((b * 2 + core) * share, 32), share)
        tile = 512

        @pl.loop(0, width // tile)
        def _(j):
            j = pl.ds(pl.multiple_of(j * tile, tile), tile)
            part[b, :, j] = jnp.dot(nt[rows, :], s2[:, j], preferred_element_type=F32).astype(BF16)

    far, plus, minus = (x + 2) % 4, (x + 1) % 4, (x + 3) % 4
    here, there = y, 1 - y
    a_cols, b_cols = slice(0, SPLIT), slice(SPLIT, width)
    half = share // 2
    copies = []

    def send(source, target, device):
        k = len(copies)
        copy = remote(source, target, r_send.at[k], r_recv.at[k], device)
        copy.start()
        copies.append(copy)
        return copy

    make_block(block(far, 0))
    a1_right = send(part.at[block(far, 0), :, a_cols], got_a1.at[0], right)
    make_block(block(far, 1))
    a1_left = send(part.at[block(far, 1), :, a_cols], got_a1.at[1], left)
    b1 = [send(part.at[block(far, there), :, b_cols], got_b1.at[far], across)]
    make_block(block(plus, there))
    b1.append(send(part.at[block(plus, there), :, b_cols], got_b1.at[plus], across))
    make_block(block(plus, here))
    a2_right = [send(part.at[block(plus, 1), :, a_cols], got_a2.at[0, 1], right)]
    make_block(block(minus, there))
    b1.append(send(part.at[block(minus, there), :, b_cols], got_b1.at[minus], across))
    make_block(block(minus, here))
    a2_left = [send(part.at[block(minus, 0), :, a_cols], got_a2.at[1, 0], left)]
    make_block(block(x, there))
    b1.append(send(part.at[block(x, there), :, b_cols], got_b1.at[x], across))
    make_block(block(x, here))

    def add_into(b, r0, r1, columns, other):
        for r in range(r0, r1, 16):
            part[b, r : r + 16, columns] = (
                part[b, r : r + 16, columns].astype(F32) + other[r - r0 : r - r0 + 16, :].astype(F32)
            ).astype(BF16)

    a1_right.wait_recv()
    add_into(block(plus, 0), 0, share, a_cols, got_a1.at[0])
    a2_right.append(send(part.at[block(plus, 0), :, a_cols], got_a2.at[0, 0], right))
    a1_left.wait_recv()
    add_into(block(minus, 1), 0, share, a_cols, got_a1.at[1])
    a2_left.append(send(part.at[block(minus, 1), :, a_cols], got_a2.at[1, 1], left))

    b1[0].wait_recv()
    add_into(block(far, here), 0, share, b_cols, got_b1.at[far])
    b2_right = send(part.at[block(far, here), :half, b_cols], got_b2.at[0], right)
    b2_left = send(part.at[block(far, here), half:, b_cols], got_b2.at[1], left)
    b1[1].wait_recv()
    add_into(block(plus, here), 0, share, b_cols, got_b1.at[plus])
    b3_right = [send(part.at[block(plus, here), half:, b_cols], got_b3.at[0, half:], right)]
    b1[2].wait_recv()
    add_into(block(minus, here), 0, share, b_cols, got_b1.at[minus])
    b3_left = [send(part.at[block(minus, here), :half, b_cols], got_b3.at[1, :half], left)]

    for copy in a2_right + a2_left:
        copy.wait_recv()
    for r in range(0, share, 16):
        rr = slice(r, r + 16)
        part[block(x, there), rr, a_cols] = (
            part[block(x, there), rr, a_cols].astype(F32)
            + got_a2[0, there, rr, :].astype(F32)
            + got_a2[1, there, rr, :].astype(F32)
        ).astype(BF16)
    a3 = send(part.at[block(x, there), :, a_cols], got_a3, across)

    b2_right.wait_recv()
    add_into(block(plus, here), 0, half, b_cols, got_b2.at[0])
    b3_right.append(send(part.at[block(plus, here), :half, b_cols], got_b3.at[0, :half], right))
    b2_left.wait_recv()
    add_into(block(minus, here), half, share, b_cols, got_b2.at[1])
    b3_left.append(send(part.at[block(minus, here), half:, b_cols], got_b3.at[1, half:], left))
    b1[3].wait_recv()

    norm = float(4096) ** (-0.5)
    for copy in b3_right + b3_left:
        copy.wait_recv()
    for r in range(0, share, 16):
        rr = slice(r, r + 16)
        wgrad[rr, b_cols] = norm * (
            part[block(x, here), rr, b_cols].astype(F32)
            + got_b1[x, rr, :].astype(F32)
            + got_b3[0, rr, :].astype(F32)
            + got_b3[1, rr, :].astype(F32)
        )
    a3.wait_recv()
    for r in range(0, share, 16):
        rr = slice(r, r + 16)
        wgrad[rr, a_cols] = norm * (
            part[block(x, here), rr, a_cols].astype(F32)
            + got_a2[0, here, rr, :].astype(F32)
            + got_a2[1, here, rr, :].astype(F32)
            + got_a3[rr, :].astype(F32)
        )

    for copy in copies:
        copy.wait_send()

    @pl.loop(0, count)
    def _(m):
        rows = rows_of(m)
        other = pl.ds(pl.multiple_of(total + m * CHUNK, CHUNK), CHUNK)
        remote(n2.at[rows, :], n2.at[other, :], n_send.at[m], n_recv.at[m], twin).wait_send()
        remote(s2.at[rows, :], s2.at[other, :], s_send.at[m], s_recv.at[m], twin).wait_send()
        for p in range(PIECES):

            @pl.when(section < sections - 1)
            def _():
                remote(
                    acts.at[rows, cols(p)], xs.at[rows, cols(p)], f_send.at[m, p], f_recv.at[m, p], after
                ).wait_send()

            @pl.when(section > 0)
            def _():
                remote(
                    grads.at[rows, cols(p)], ds_in.at[rows, cols(p)], b_send.at[m, p], b_recv.at[m, p], before
                ).wait_send()


def body(inputs, cotangent, weight, gain):
    micro, tokens, width = inputs.shape
    total = micro * tokens
    share = width // lax.axis_size("dp")
    count = total // CHUNK
    rest = width - SPLIT
    half = share // 2
    vmem, dma = pltpu.VMEM, pltpu.SemaphoreType.DMA
    acts, grads, wgrad = pl.pallas_call(
        kernel,
        out_shape=(
            jax.ShapeDtypeStruct((total, width), BF16),
            jax.ShapeDtypeStruct((total, width), BF16),
            jax.ShapeDtypeStruct((share, width), F32),
        ),
        in_specs=[pl.BlockSpec(memory_space=pl.ANY)] * 3 + [pl.BlockSpec(memory_space=vmem)],
        out_specs=[pl.BlockSpec(memory_space=vmem)] * 3,
        scratch_shapes=[
            vmem((width, width), BF16),
            vmem((width, width), BF16),
            vmem((total, width), BF16),
            vmem((total, width), BF16),
            vmem((total, width), F32),
            vmem((total, 128), F32),
            vmem((CHUNK, width), F32),
            vmem((2 * total, width), BF16),
            vmem((2 * total, width), BF16),
            vmem((width, 2 * total), BF16),
            vmem((8, share, width), BF16),
            vmem((2, share, SPLIT), BF16),
            vmem((2, 2, share, SPLIT), BF16),
            vmem((share, SPLIT), BF16),
            vmem((4, share, rest), BF16),
            vmem((2, half, rest), BF16),
            vmem((2, share, rest), BF16),
            dma((PIECES,)),
            dma((count, PIECES)),
            dma((count, PIECES)),
            dma((count, PIECES)),
            dma((count, PIECES)),
            dma((count,)),
            dma((count,)),
            dma((count,)),
            dma((count,)),
            dma((17,)),
            dma((17,)),
        ],
        compiler_params=pltpu.CompilerParams(
            collective_id=0, has_side_effects=True, vmem_limit_bytes=60 * 1024 * 1024
        ),
    )(inputs.reshape(total, width), cotangent.reshape(total, width), weight[0], gain)
    shape = (1, micro, tokens, width)
    return (acts.reshape(shape), grads.reshape(shape), wgrad[None])


def solution(mesh):
    in_specs = (
        P(None, "dp", None),
        P(None, "dp", None),
        P("section", None, None),
        P("section", None),
    )
    out_specs = (
        P("section", None, "dp", None),
        P("section", None, "dp", None),
        P("section", "dp", None),
    )
    return jax.shard_map(body, mesh=mesh, in_specs=in_specs, out_specs=out_specs, check_vma=False)
```

time: 785 us -> 244 us (0.31)
  waiting for transfers between devices: 567 us -> 0 us
  Pallas kernels: 0 us -> 238 us
  starting transfers between devices: 99.4 us -> 0 us
  matrix products: 72.5 us -> 0 us
  other arithmetic: 21.2 us -> 0 us
  between operations: 14.1 us -> 0.65 us
    psum x1 -> x0, waiting for transfers between devices: 316 us -> none  [body(): total = lax.psum(local_grad.astype(jnp.bfloat16), 'dp').astype(jnp.float32)]
    ppermute x22 -> x0, waiting for transfers between devices: 251 us -> none  [passed_along(): return lax.ppermute(array, axis, pairs)]
    pallas_call x0 -> x1, Pallas kernels: none -> 238 us  [body(): pl.pallas_call(kernel, out_shape=(jax.ShapeDtypeStruct((total, width), BF...]
    ppermute x22 -> x0, starting transfers between devices: 99.3 us -> none  [passed_along(): return lax.ppermute(array, axis, pairs)]
    dot_general x9 -> x0, matrix products: 72.5 us -> none  [the longest x4 35.5 us: backward_active(): lax.dot_general(slope, w_local, (((1,), (1,)), ((), ())), preferred_eleme...]
    dynamic_update_slice x12 -> x0, other arithmetic: 16.6 us -> none  [put_row(): return lax.dynamic_update_index_in_dim(buffer, value, index, 0)]
  transfers between devices with their start and end apart: 23 -> 0, of which waited for: 23 -> 0; matrix products, arithmetic and copies ran while one was open for 0% -> 0% of each run, Pallas kernels for 0% -> 0%
where the time goes in v1:
time: 244 us
  Pallas kernels  238 us (98%)
  local copies, waits for them, and re-layouts  5.63 us (2%)
    pallas_call x1, Pallas kernels, body(): pl.pallas_call(kernel, out_shape=(jax.ShapeDtypeStruct((total, width), BF...  238 us
    unnamed x7, local copies, waits for them, and re-layouts  5.63 us

profile of v1, /device:TPU:1, one launch (start us, length us, event | category | flops | bytes accessed | tf_op | source)
XLA Modules:
  0.0 243.8 jit_solution(7738424764569124751)
XLA Ops:
  0.6 237.5 %shard_map.67 = (bf16[256,2560]{1,0:T(8,128)(2,1)}, bf16[256,2560]{1,0:T(8,128)(2,1)}, f32[160,2560]{1,0:T(8,128)}) custom-call(bf16[256,2560]{1,0:T(8,128)(2,1)} %bitcast.10, bf16[256,2560]{1,0:T(8,128)(2,1)} %bitcast.11, bf16[2560,2560]{1,0:T(8,128)(2,1)} %bitcast.6, f32[1,2560]{1,0:T(1,128)} %gain.1), custom_call_target="tpu_custom_call" | custom-call | tf_op jit(solution)/shard_map/pallas_call | solution.py:351
  238.2 0.0 copy-start.1
  238.2 2.6 %copy.10 = bf16[1,4,64,2560]{3,2,1,0:T(8,128)(2,1)} copy(bf16[1,4,64,2560]{3,2,1,0:T(8,128)(2,1)} %bitcast.9) | data formatting | bytes 2621440
  240.7 0.0 copy-done.1
  240.7 0.0 copy-start
  240.7 1.1 copy.11
  241.8 0.8 copy-done
  242.6 1.2 copy.12
Async XLA Ops:
  238.2 2.6 %copy-start.1 = (bf16[256,2560]{1,0:T(8,128)(2,1)S(1)}, bf16[256,2560]{1,0:T(8,128)(2,1)}, u32[]{:S(2)}) copy-start(bf16[256,2560]{1,0:T(8,128)(2,1)} %get-tuple-element.7) | copy-start | bytes 3932164
  240.7 1.9 copy-start

commit v2 on v1

v2 whole, which is shorter than its diff:
```python
import jax
import jax.numpy as jnp
from jax import lax
from jax.experimental import pallas as pl
from jax.experimental.pallas import tpu as pltpu
from jax.sharding import PartitionSpec as P

EPS = 1e-05
MESH = pl.DeviceIdType.MESH
BF16, F32 = jnp.bfloat16, jnp.float32

CHUNK = 16
PIECES = 5
GROUP = 64
AHEAD = 7
QUARTERS = 4


def kernel(
    x_hbm, d_hbm, w_hbm, gain, acts_out, grads_out, wgrad_out,
    w_v, wt_v, xs, ds_in, acts, grads, pre, rinv, acc, normed, nx, nt, sx, total_p,
    to_twin, from_twin, to_across, from_across, wgrad,
    w_sem, x_sem, d_sem, out_sem, f_send, f_recv, b_send, b_recv, n_send, n_recv, s_send, s_recv,
    t_send, t_recv, y_send, y_recv,
):
    total, width = xs.shape
    count = total // CHUNK
    piece = width // PIECES
    window = nt.shape[0]
    share = wgrad.shape[0]
    quarter = width // QUARTERS
    ways = window // share
    per_group = GROUP // CHUNK
    groups = total // GROUP
    deep = 4 * GROUP
    section, dp = lax.axis_index("section"), lax.axis_index("dp")
    sections = lax.axis_size("section")
    x, y, core = dp // 4, (dp // 2) % 2, dp % 2
    first, last = section == 0, section == sections - 1
    early = section >= sections // 2

    def at(x_to, y_to, core_to):
        return (section, x_to * 4 + y_to * 2 + core_to)

    after, before = (section + 1, dp), (section - 1, dp)
    twin, across = at(x, y, 1 - core), at(x, 1 - y, core)
    steps = (1, 3, 2)
    others = [(x + step) % 4 for step in steps]

    def local(source, target, sem):
        return pltpu.make_async_copy(source, target, sem)

    def remote(source, target, send, recv, device):
        return pltpu.make_async_remote_copy(
            src_ref=source, dst_ref=target, send_sem=send, recv_sem=recv, device_id=device, device_id_type=MESH
        )

    def cols(p):
        return slice(p * piece, (p + 1) * piece)

    def rows_of(m):
        return pl.ds(pl.multiple_of(m * CHUNK, CHUNK), CHUNK)

    def slot(m, source):
        start = (m // per_group) * deep + source * GROUP + (m % per_group) * CHUNK
        return pl.ds(pl.multiple_of(start, CHUNK), CHUNK)

    def fetch_x(p):
        return local(x_hbm.at[:, cols(p)], xs.at[:, cols(p)], x_sem.at[p])

    def fetch_d(p):
        return local(d_hbm.at[:, cols(p)], ds_in.at[:, cols(p)], d_sem.at[p])

    def fetch_w(p):
        return local(w_hbm.at[cols(p), :], w_v.at[cols(p), :], w_sem.at[p])

    def push_acts(m, p):
        here = (rows_of(m), cols(p))
        return remote(acts.at[here], xs.at[here], f_send.at[m, p], f_recv.at[m, p], after)

    def push_grads(m, p):
        here = (rows_of(m), cols(p))
        return remote(grads.at[here], ds_in.at[here], b_send.at[m, p], b_recv.at[m, p], before)

    def push_normed(m, k):
        part = pl.ds(pl.multiple_of(others[k] * window, 128), window)
        return remote(
            normed.at[rows_of(m), part], nx.at[slot(m, x), :], n_send.at[k, m], n_recv.at[k, m], at(others[k], y, core)
        )

    def push_s(m, k):
        here = sx.at[slot(m, x), :]
        return remote(here, here, s_send.at[k, m], s_recv.at[k, m], at(others[k], y, core))

    def keep_acts(m):
        return local(acts.at[rows_of(m), :], acts_out.at[rows_of(m), :], out_sem.at[0, m])

    def keep_grads(m):
        return local(grads.at[rows_of(m), :], grads_out.at[rows_of(m), :], out_sem.at[1, m])

    @pl.when(first)
    def _():
        for p in range(PIECES):
            fetch_x(p).start()

    for p in range(PIECES):
        fetch_w(p).start()

    @pl.when(last)
    def _():
        for p in range(PIECES):
            fetch_d(p).start()

    barrier = pltpu.get_barrier_semaphore()
    for device in [twin, across] + [at(other, y, core) for other in others]:
        pl.semaphore_signal(barrier, inc=1, device_id=device, device_id_type=MESH)

    @pl.when(section > 0)
    def _():
        pl.semaphore_signal(barrier, inc=1, device_id=before, device_id_type=MESH)

    @pl.when(section < sections - 1)
    def _():
        pl.semaphore_signal(barrier, inc=1, device_id=after, device_id_type=MESH)

    pl.semaphore_wait(barrier, 5 + (section > 0).astype(jnp.int32) + (section < sections - 1).astype(jnp.int32))

    def turn_weight():
        tile = 256

        @pl.loop(0, width // tile)
        def _(i):
            i = pl.ds(pl.multiple_of(i * tile, tile), tile)
            for j in range(0, width, tile):
                wt_v[j : j + tile, i] = w_v[i, j : j + tile].T

    def turn_normed():
        for k in range(3):

            @pl.loop(0, count)
            def _(m):
                push_normed(m, k).wait_recv()

        @pl.loop(0, groups)
        def _(g):
            g = pl.ds(pl.multiple_of(g * deep, deep), deep)
            nt[:, g] = nx[g, :].T

        @pl.loop(0, window // 16)
        def _(i):
            i = pl.ds(pl.multiple_of(i * 16, 16), 16)
            total_p[i, :] = jnp.zeros((16, width), F32)

    def await_group(g):
        for k in range(3):
            for i in range(per_group):
                push_s(g * per_group + i, k).wait_recv()

    def add_group(g):
        await_group(g)
        g = pl.ds(pl.multiple_of(g * deep, deep), deep)
        tile = 512

        @pl.loop(0, width // tile)
        def _(j):
            j = pl.ds(pl.multiple_of(j * tile, tile), tile)
            total_p[:, j] += jnp.dot(nt[:, g], sx[g, j], preferred_element_type=F32)

    @pl.when(early)
    def _():
        for p in range(PIECES):
            fetch_w(p).wait()
        turn_weight()

    def add_product(lhs, rhs, p):
        tile = 512
        for j in range(0, width, tile):
            term = jnp.dot(lhs, rhs[cols(p), j : j + tile], preferred_element_type=F32)
            if p == 0:
                acc[:, j : j + tile] = term
            else:
                acc[:, j : j + tile] += term

    def lane_sum(values):
        out = values[:, :128]
        for j in range(128, values.shape[1], 128):
            out = out + values[:, j : j + 128]
        return out

    def forward(m):
        rows = rows_of(m)
        squares = None
        for p in range(PIECES):

            @pl.when(section > 0)
            def _():
                local(xs.at[rows, cols(p)], xs.at[rows, cols(p)], f_recv.at[m, p]).wait()

            @pl.when(jnp.logical_and(m == 0, first))
            def _():
                fetch_x(p).wait()

            @pl.when(jnp.logical_and(m == 0, jnp.logical_not(early)))
            def _():
                fetch_w(p).wait()

            xf = xs[rows, cols(p)].astype(F32)
            term = lane_sum(xf * xf)
            squares = term if squares is None else squares + term
            add_product((xf * gain[:, cols(p)]).astype(BF16), w_v, p)
        r = lax.rsqrt(jnp.sum(squares, -1, keepdims=True) * (1.0 / width) + EPS)
        for p in range(PIECES):
            a = acc[:, cols(p)] * r
            pre[rows, cols(p)] = a
            acts[rows, cols(p)] = (xs[rows, cols(p)].astype(F32) + a * jax.nn.sigmoid(a)).astype(BF16)

            @pl.when(section < sections - 1)
            def _():
                push_acts(m, p).start()

        keep_acts(m).start()
        rinv[rows, :] = jnp.broadcast_to(r, (CHUNK, 128))
        for p in range(PIECES):
            normed[rows, cols(p)] = (xs[rows, cols(p)].astype(F32) * r * gain[:, cols(p)]).astype(BF16)
        nx[slot(m, x), :] = normed[rows, pl.ds(pl.multiple_of(x * window, 128), window)]
        for k in range(3):
            push_normed(m, k).start()

    def backward(m):
        rows = rows_of(m)
        dots = None
        for p in range(PIECES):
            a = pre[rows, cols(p)]
            sig = jax.nn.sigmoid(a)
            slope = sig * (1.0 + a * (1.0 - sig))

            @pl.when(section < sections - 1)
            def _():
                local(ds_in.at[rows, cols(p)], ds_in.at[rows, cols(p)], b_recv.at[m, p]).wait()

            @pl.when(jnp.logical_and(m == 0, last))
            def _():
                fetch_d(p).wait()

            s = (ds_in[rows, cols(p)].astype(F32) * slope).astype(BF16)
            sx[slot(m, x), cols(p)] = s
            term = lane_sum(s.astype(F32) * a)
            dots = term if dots is None else dots + term
            add_product(s, wt_v, p)
        r = rinv[rows, :1]
        scale = r * r * (jnp.sum(dots, -1, keepdims=True) * (1.0 / width))
        for p in range(PIECES):
            out = (
                ds_in[rows, cols(p)].astype(F32)
                + r * (gain[:, cols(p)] * acc[:, cols(p)])
                - xs[rows, cols(p)].astype(F32) * scale
            )
            grads[rows, cols(p)] = out.astype(BF16)

            @pl.when(section > 0)
            def _():
                push_grads(m, p).start()

        for k in range(3):
            push_s(m, k).start()
        keep_grads(m).start()

    behind = sections - 1 - section
    warm = jnp.minimum(count, AHEAD * behind + (behind > 0).astype(jnp.int32))

    @pl.loop(0, 2 * count)
    def _(i):
        @pl.when(i < count)
        def _():
            forward(i)

        @pl.when(jnp.logical_and(i == count - 1, jnp.logical_not(early)))
        def _():
            turn_weight()
            turn_normed()

        m = i - warm

        @pl.when(jnp.logical_and(m >= 0, m < count))
        def _():
            backward(m)

        done = m // per_group - 1

        @pl.when(jnp.logical_and(jnp.logical_not(early), jnp.logical_and(m % per_group == per_group - 1, done >= 0)))
        def _():
            add_group(done)

    @pl.when(early)
    def _():
        turn_normed()

        @pl.loop(0, groups - 1)
        def _(g):
            add_group(g)

    await_group(groups - 1)
    tail = slice((groups - 1) * deep, groups * deep)

    def quarter_of(q):
        return pl.ds(pl.multiple_of(q * quarter, 128), quarter)

    def finished(y_to, core_to, q):
        rows = pl.ds(pl.multiple_of((y_to * 2 + core_to) * share, 32), share)
        return total_p[rows, q] + jnp.dot(nt[rows, tail], sx[tail, q], preferred_element_type=F32)

    def push_twin(k, q):
        return remote(
            to_twin.at[k, :, quarter_of(q)], from_twin.at[k, :, quarter_of(q)], t_send.at[k, q], t_recv.at[k, q], twin
        )

    def push_across(q):
        return remote(
            to_across.at[:, quarter_of(q)], from_across.at[:, quarter_of(q)], y_send.at[q], y_recv.at[q], across
        )

    def keep_wgrad(q):
        return local(wgrad.at[:, quarter_of(q)], wgrad_out.at[:, quarter_of(q)], out_sem.at[2, q])

    norm = float(4096) ** (-0.5)

    @pl.loop(0, QUARTERS)
    def _(q):
        to_twin[0, :, quarter_of(q)] = finished(1 - y, 1 - core, quarter_of(q)).astype(BF16)
        push_twin(0, q).start()

    @pl.loop(0, QUARTERS)
    def _(q):
        value = finished(1 - y, core, quarter_of(q))
        push_twin(0, q).wait_recv()
        to_across[:, quarter_of(q)] = (value + from_twin[0, :, quarter_of(q)].astype(F32)).astype(BF16)
        push_across(q).start()

    @pl.loop(0, QUARTERS)
    def _(q):
        to_twin[1, :, quarter_of(q)] = finished(y, 1 - core, quarter_of(q)).astype(BF16)
        push_twin(1, q).start()

    @pl.loop(0, QUARTERS)
    def _(q):
        value = finished(y, core, quarter_of(q))
        push_twin(1, q).wait_recv()
        wgrad[:, quarter_of(q)] = value + from_twin[1, :, quarter_of(q)].astype(F32)

    @pl.loop(0, QUARTERS)
    def _(q):
        push_across(q).wait_recv()
        wgrad[:, quarter_of(q)] = norm * (wgrad[:, quarter_of(q)] + from_across[:, quarter_of(q)].astype(F32))
        keep_wgrad(q).start()

    @pl.loop(0, QUARTERS)
    def _(q):
        push_twin(0, q).wait_send()
        push_twin(1, q).wait_send()
        push_across(q).wait_send()

    @pl.loop(0, count)
    def _(m):
        for k in range(3):
            push_normed(m, k).wait_send()
            push_s(m, k).wait_send()
        keep_acts(m).wait()
        keep_grads(m).wait()
        for p in range(PIECES):

            @pl.when(section < sections - 1)
            def _():
                push_acts(m, p).wait_send()

            @pl.when(section > 0)
            def _():
                push_grads(m, p).wait_send()

    @pl.loop(0, QUARTERS)
    def _(q):
        keep_wgrad(q).wait()


def place(acts_in, grads_in, wgrad_in, acts, grads, wgrad, held, held_wide, in_sems, out_sems):
    parts = 4
    loads, stores = [], []
    arrays = ((acts_in, held.at[0], acts), (grads_in, held.at[1], grads), (wgrad_in, held_wide, wgrad))
    for k, (source, middle, target) in enumerate(arrays):
        step = source.shape[0] // parts
        for i in range(parts):
            rows = slice(i * step, (i + 1) * step)
            loads.append(pltpu.make_async_copy(source.at[rows, :], middle.at[rows, :], in_sems.at[k, i]))
            stores.append(pltpu.make_async_copy(middle.at[rows, :], target.at[rows, :], out_sems.at[k, i]))
    for load in loads:
        load.start()
    for load, store in zip(loads, stores):
        load.wait()
        store.start()
    for store in stores:
        store.wait()


def body(inputs, cotangent, weight, gain):
    micro, tokens, width = inputs.shape
    total = micro * tokens
    share = width // lax.axis_size("dp")
    window = 4 * share
    count = total // CHUNK
    vmem, dma = pltpu.VMEM, pltpu.SemaphoreType.DMA
    anywhere = pl.BlockSpec(memory_space=pl.ANY)
    shapes = (
        jax.ShapeDtypeStruct((total, width), BF16),
        jax.ShapeDtypeStruct((total, width), BF16),
        jax.ShapeDtypeStruct((share, width), F32),
    )
    results = pl.pallas_call(
        kernel,
        out_shape=shapes,
        in_specs=[anywhere] * 3 + [pl.BlockSpec(memory_space=vmem)],
        out_specs=[anywhere] * 3,
        scratch_shapes=[
            vmem((width, width), BF16),
            vmem((width, width), BF16),
            vmem((total, width), BF16),
            vmem((total, width), BF16),
            vmem((total, width), BF16),
            vmem((total, width), BF16),
            vmem((total, width), F32),
            vmem((total, 128), F32),
            vmem((CHUNK, width), F32),
            vmem((total, width), BF16),
            vmem((4 * total, window), BF16),
            vmem((window, 4 * total), BF16),
            vmem((4 * total, width), BF16),
            vmem((window, width), F32),
            vmem((2, share, width), BF16),
            vmem((2, share, width), BF16),
            vmem((share, width), BF16),
            vmem((share, width), BF16),
            vmem((share, width), F32),
            dma((PIECES,)),
            dma((PIECES,)),
            dma((PIECES,)),
            dma((3, count)),
            dma((count, PIECES)),
            dma((count, PIECES)),
            dma((count, PIECES)),
            dma((count, PIECES)),
            dma((3, count)),
            dma((3, count)),
            dma((3, count)),
            dma((3, count)),
            dma((2, QUARTERS)),
            dma((2, QUARTERS)),
            dma((QUARTERS,)),
            dma((QUARTERS,)),
        ],
        compiler_params=pltpu.CompilerParams(
            collective_id=0, has_side_effects=True, vmem_limit_bytes=62 * 1024 * 1024
        ),
    )(inputs.reshape(total, width), cotangent.reshape(total, width), weight[0], gain)
    acts, grads, wgrad = pl.pallas_call(
        place,
        out_shape=shapes,
        in_specs=[anywhere] * 3,
        out_specs=[anywhere] * 3,
        scratch_shapes=[vmem((2, total, width), BF16), vmem((share, width), F32), dma((3, 4)), dma((3, 4))],
        compiler_params=pltpu.CompilerParams(vmem_limit_bytes=62 * 1024 * 1024),
    )(*results)
    shape = (1, micro, tokens, width)
    return (acts.reshape(shape), grads.reshape(shape), wgrad[None])


def solution(mesh):
    in_specs = (
        P(None, "dp", None),
        P(None, "dp", None),
        P("section", None, None),
        P("section", None),
    )
    out_specs = (
        P("section", None, "dp", None),
        P("section", None, "dp", None),
        P("section", "dp", None),
    )
    return jax.shard_map(body, mesh=mesh, in_specs=in_specs, out_specs=out_specs, check_vma=False)
```

time: 244 us -> 184 us (0.75)
  Pallas kernels: 238 us -> 184 us
  local copies, waits for them, and re-layouts: 5.63 us -> 0 us
    pallas_call x1 -> x2, Pallas kernels: 238 us -> 184 us  [the longest x1 180 us: body(): pl.pallas_call(kernel, out_shape=shapes, in_specs=[anywhere] * 3 + [pl.Bl...]
    unnamed x7 -> x0, local copies, waits for them, and re-layouts: 5.63 us -> none
where the time goes in v2:
time: 184 us
  Pallas kernels  184 us (100%)
    pallas_call x1, Pallas kernels, body(): pl.pallas_call(kernel, out_shape=shapes, in_specs=[anywhere] * 3 + [pl.Bl...  180 us
    pallas_call x1, Pallas kernels, body(): pl.pallas_call(place, out_shape=shapes, in_specs=[anywhere] * 3, out_spec...  3.86 us

profile of v2, /device:TPU:1, one launch (start us, length us, event | category | flops | bytes accessed | tf_op | source)
XLA Modules:
  0.0 184.2 jit_solution(5657180144121347966)
XLA Ops:
  0.6 179.7 %shard_map.67 = (bf16[256,2560]{1,0:T(8,128)(2,1)}, bf16[256,2560]{1,0:T(8,128)(2,1)}, f32[160,2560]{1,0:T(8,128)}) custom-call(bf16[256,2560]{1,0:T(8,128)(2,1)} %bitcast.7, bf16[256,2560]{1,0:T(8,128)(2,1)} %bitcast.8, bf16[2560,2560]{1,0:T(8,128)(2,1)} %bitcast.6, f32[1,2560]{1,0:T(1,128)} %gain.1), custom_call_target="tpu_custom_call" | custom-call | tf_op jit(solution)/shard_map/pallas_call | solution.py:416
  180.4 3.9 %shard_map.68 = (bf16[256,2560]{1,0:T(8,128)(2,1)}, bf16[256,2560]{1,0:T(8,128)(2,1)}, f32[160,2560]{1,0:T(8,128)}) custom-call(bf16[256,2560]{1,0:T(8,128)(2,1)} %get-tuple-element.9.acts_in, bf16[256,2560]{1,0:T(8,128)(2,1)} %get-tuple-element.10.grads_in, f32[160,2560]{1,0:T(8,128)} %get-tuple-element.11.wgrad_in), custom_call_target="tpu_custom_call" | custom-call | tf_op jit(solution)/shard_map/pallas_call | solution.py:462

commit v3 on v2

v3 whole, which is shorter than its diff:
```python
import jax
import jax.numpy as jnp
from jax import lax
from jax.experimental import pallas as pl
from jax.experimental.pallas import tpu as pltpu
from jax.sharding import PartitionSpec as P

EPS = 1e-05
MESH = pl.DeviceIdType.MESH
BF16, F32 = jnp.bfloat16, jnp.float32

CHUNK = 16
PIECES = 5
GROUP = 64
PAIRED = 2
SINGLES = 2
AHEAD = 3
BLOCKS = ((0, 1), (2, 3, 4))
PADDED = 128


def kernel(
    x_hbm, d_hbm, w_hbm, gain, acts_out, grads_out, wgrad_out,
    w_v, wt_v, xs, ds_in, acts, grads, pre, rinv, acc, slopes, nx, nt, sx, partial,
    to_twin, from_twin, to_across, from_across, to_x, from_x, wgrad,
    w_sem, out_sem, f_send, f_recv, b_send, b_recv, n_send, n_recv, s_send, s_recv,
    t_send, t_recv, y_send, y_recv, o_send, o_recv,
):
    total, width = xs.shape
    count = total // CHUNK
    piece = width // PIECES
    window = sx.shape[1]
    share = wgrad.shape[0]
    per_group = GROUP // CHUNK
    groups = total // GROUP
    deep = 4 * GROUP
    section, dp = lax.axis_index("section"), lax.axis_index("dp")
    sections = lax.axis_size("section")
    x, y, core = dp // 4, (dp // 2) % 2, dp % 2
    first, last = section == 0, section == sections - 1
    early = section >= sections // 2

    def at(x_to, y_to, core_to):
        return (section, x_to * 4 + y_to * 2 + core_to)

    after, before = (section + 1, dp), (section - 1, dp)
    twin, across = at(x, y, 1 - core), at(x, 1 - y, core)
    steps = (1, 3, 2)
    others = [(x + step) % 4 for step in steps]

    def local(source, target, sem):
        return pltpu.make_async_copy(source, target, sem)

    def remote(source, target, send, recv, device):
        return pltpu.make_async_remote_copy(
            src_ref=source, dst_ref=target, send_sem=send, recv_sem=recv, device_id=device, device_id_type=MESH
        )

    def cols(p):
        return slice(p * piece, (p + 1) * piece)

    def rows_of(m, n=1):
        return pl.ds(pl.multiple_of(m * CHUNK, CHUNK), n * CHUNK)

    def slot(m, source, n=1):
        start = (m // per_group) * deep + source * GROUP + (m % per_group) * CHUNK
        return pl.ds(pl.multiple_of(start, CHUNK), n * CHUNK)

    def window_of(owner):
        return pl.ds(pl.multiple_of(owner * window, 128), window)

    def fetch_x(m):
        for p in range(PIECES):
            here = (rows_of(m), cols(p))
            local(x_hbm.at[here], xs.at[here], f_recv.at[m, p]).start()

    def fetch_d(m):
        for p in range(PIECES):
            here = (rows_of(m), cols(p))
            local(d_hbm.at[here], ds_in.at[here], b_recv.at[m, p]).start()

    def fetch_w(p):
        return local(w_hbm.at[cols(p), :], w_v.at[cols(p), :], w_sem.at[p])

    def push_acts(m, p):
        here = (rows_of(m), cols(p))
        return remote(acts.at[here], xs.at[here], f_send.at[m, p], f_recv.at[m, p], after)

    def push_grads(m, p):
        here = (rows_of(m), cols(p))
        return remote(grads.at[here], ds_in.at[here], b_send.at[m, p], b_recv.at[m, p], before)

    def push_normed(m, k):
        here = nx.at[slot(m, x), :]
        return remote(here, here, n_send.at[k, m], n_recv.at[k, m], at(others[k], y, core))

    def push_s(m, k):
        return remote(
            slopes.at[rows_of(m), window_of(others[k])],
            sx.at[slot(m, x), :],
            s_send.at[k, m],
            s_recv.at[k, m],
            at(others[k], y, core),
        )

    def keep_acts(m):
        return local(acts.at[rows_of(m), :], acts_out.at[rows_of(m), :], out_sem.at[0, m])

    def keep_grads(m):
        return local(grads.at[rows_of(m), :], grads_out.at[rows_of(m), :], out_sem.at[1, m])

    @pl.when(first)
    def _():
        fetch_x(0)

    for p in range(PIECES):
        fetch_w(p).start()

    @pl.when(first)
    def _():
        fetch_x(1)

    @pl.when(last)
    def _():
        @pl.loop(0, count)
        def _(m):
            fetch_d(m)

    barrier = pltpu.get_barrier_semaphore()
    for device in [twin, across] + [at(other, y, core) for other in others]:
        pl.semaphore_signal(barrier, inc=1, device_id=device, device_id_type=MESH)

    @pl.when(section > 0)
    def _():
        pl.semaphore_signal(barrier, inc=1, device_id=before, device_id_type=MESH)

    @pl.when(section < sections - 1)
    def _():
        pl.semaphore_signal(barrier, inc=1, device_id=after, device_id_type=MESH)

    pl.semaphore_wait(barrier, 5 + (section > 0).astype(jnp.int32) + (section < sections - 1).astype(jnp.int32))

    def turn_weight():
        tile = 256

        @pl.loop(0, width // tile)
        def _(i):
            i = pl.ds(pl.multiple_of(i * tile, tile), tile)
            for j in range(0, width, tile):
                wt_v[j : j + tile, i] = w_v[i, j : j + tile].T

    def turn_normed():
        for k in range(3):

            @pl.loop(0, count)
            def _(m):
                push_normed(m, k).wait_recv()

        tile = 256

        @pl.loop(0, width // tile)
        def _(i):
            i = pl.ds(pl.multiple_of(i * tile, tile), tile)
            for g in range(groups):
                g = slice(g * deep, (g + 1) * deep)
                nt[i, g] = nx[g, i].T

    def await_group(g):
        for k in range(3):
            for i in range(per_group):
                push_s(g * per_group + i, k).wait_recv()

    @pl.when(jnp.logical_not(first))
    def _():
        for p in range(PIECES):
            fetch_w(p).wait()

    @pl.when(early)
    def _():
        turn_weight()

    def add_product(lhs, rhs, p, taken):
        tile = 512
        if taken > CHUNK:
            lhs = jnp.concatenate([lhs, jnp.zeros((PADDED - taken, piece), BF16)], 0)
        for j in range(0, width, tile):
            term = jnp.dot(lhs, rhs[cols(p), j : j + tile], preferred_element_type=F32)[:taken]
            if p == 0:
                acc[:taken, j : j + tile] = term
            else:
                acc[:taken, j : j + tile] += term

    def lane_sum(values):
        out = values[:, :128]
        for j in range(128, values.shape[1], 128):
            out = out + values[:, j : j + 128]
        return out

    def forward(m, n, cold=False):
        rows = rows_of(m, n)
        taken = n * CHUNK
        squares = None
        for p in range(PIECES):

            for i in range(n):
                here = xs.at[rows_of(m + i), cols(p)]
                local(here, here, f_recv.at[m + i, p]).wait()
            if cold:
                fetch_w(p).wait()
            xf = xs[rows, cols(p)].astype(F32)
            term = lane_sum(xf * xf)
            squares = term if squares is None else squares + term
            add_product((xf * gain[:, cols(p)]).astype(BF16), w_v, p, taken)
        r = lax.rsqrt(jnp.sum(squares, -1, keepdims=True) * (1.0 / width) + EPS)
        for block in BLOCKS:
            for p in block:
                a = acc[:taken, cols(p)] * r
                pre[rows, cols(p)] = a
                acts[rows, cols(p)] = (xs[rows, cols(p)].astype(F32) + a * jax.nn.sigmoid(a)).astype(BF16)

            @pl.when(section < sections - 1)
            def _():
                for i in range(n):
                    for p in block:
                        push_acts(m + i, p).start()

        if n == 1:

            @pl.when(jnp.logical_and(first, m + 2 < count))
            def _():
                fetch_x(m + 2)

        rinv[rows, :] = jnp.broadcast_to(r, (taken, 128))
        for p in range(PIECES):
            nx[slot(m, x, n), cols(p)] = (xs[rows, cols(p)].astype(F32) * r * gain[:, cols(p)]).astype(BF16)
        for i in range(n):
            keep_acts(m + i).start()
            for k in range(3):
                push_normed(m + i, k).start()

    def backward(m, n):
        rows = rows_of(m, n)
        taken = n * CHUNK
        dots = None
        for p in range(PIECES):
            a = pre[rows, cols(p)]
            sig = jax.nn.sigmoid(a)
            slope = sig * (1.0 + a * (1.0 - sig))

            for i in range(n):
                here = ds_in.at[rows_of(m + i), cols(p)]
                local(here, here, b_recv.at[m + i, p]).wait()
            s = (ds_in[rows, cols(p)].astype(F32) * slope).astype(BF16)
            slopes[rows, cols(p)] = s
            term = lane_sum(s.astype(F32) * a)
            dots = term if dots is None else dots + term
            add_product(s, wt_v, p, taken)

        def share_s():
            for i in range(n):
                for k in range(3):
                    push_s(m + i, k).start()

        r = rinv[rows, :1]
        scale = r * r * (jnp.sum(dots, -1, keepdims=True) * (1.0 / width))
        for block in BLOCKS:
            for p in block:
                out = (
                    ds_in[rows, cols(p)].astype(F32)
                    + r * (gain[:, cols(p)] * acc[:taken, cols(p)])
                    - xs[rows, cols(p)].astype(F32) * scale
                )
                grads[rows, cols(p)] = out.astype(BF16)

            @pl.when(section > 0)
            def _():
                for i in range(n):
                    for p in block:
                        push_grads(m + i, p).start()

        share_s()
        sx[slot(m, x, n), :] = slopes[rows, window_of(x)]
        for i in range(n):
            keep_grads(m + i).start()

    behind = sections - 1 - section
    paired = behind < PAIRED
    pairs = (count - 2 * SINGLES) // 2
    lag = jnp.where(paired, AHEAD * behind, count)

    def visit(step, paired, work, skip):
        inside = jnp.logical_and(step >= SINGLES, step < SINGLES + pairs)
        two = jnp.logical_and(paired, inside)
        start = jnp.where(step < SINGLES, step, jnp.where(inside, 2 * step - SINGLES, step + pairs))
        start = jnp.where(paired, start, step)
        active = jnp.logical_and(step >= skip, step < jnp.where(paired, pairs + 2 * SINGLES, count))

        @pl.when(jnp.logical_and(active, two))
        def _():
            work(start, 2)

        @pl.when(jnp.logical_and(active, jnp.logical_not(two)))
        def _():
            work(start, 1)

    @pl.when(first)
    def _():
        forward(0, 1, cold=True)

    @pl.loop(0, 2 * count)
    def _(i):
        visit(i, paired, forward, first.astype(jnp.int32))

        @pl.when(jnp.logical_and(i == count - 1, jnp.logical_not(early)))
        def _():
            turn_weight()
            turn_normed()

        visit(i - lag, paired, backward, 0)

    @pl.when(early)
    def _():
        turn_normed()

    def owner(k):
        step = jnp.where(k == 0, 2, jnp.where(k == 1, 1, jnp.where(k == 2, 3, 0)))
        return (x + step) % 4

    def product(k, y_to, core_to, tokens):
        start = owner(k) * (4 * share) + (y_to * 2 + core_to) * share
        rows = pl.ds(pl.multiple_of(start, 32), share)
        return jnp.dot(nt[rows, tokens], sx[tokens, :], preferred_element_type=F32)

    known, tail = slice(0, (groups - 1) * deep), slice((groups - 1) * deep, groups * deep)
    for g in range(groups - 1):
        await_group(g)

    @pl.loop(0, 4)
    def _(k):
        partial[0, k] = product(k, 1 - y, 1 - core, known)
        partial[1, k] = product(k, 1 - y, core, known)

    await_group(groups - 1)

    def push_twin(half, k):
        return remote(to_twin.at[half, k], from_twin.at[half, k], t_send.at[half, k], t_recv.at[half, k], twin)

    def push_across(k):
        return remote(to_across.at[k], from_across.at[k], y_send.at[k], y_recv.at[k], across)

    def push_owner(k):
        return remote(to_x.at[k], from_x.at[k], o_send.at[k], o_recv.at[k], at(owner(k), y, core))

    def keep_wgrad(source):
        return local(wgrad.at[:, window_of(source)], wgrad_out.at[:, window_of(source)], out_sem.at[2, source])

    norm = float(4096) ** (-0.5)

    @pl.loop(0, 4)
    def _(k):
        to_twin[0, k] = (partial[0, k] + product(k, 1 - y, 1 - core, tail)).astype(BF16)
        push_twin(0, k).start()

    @pl.loop(0, 4)
    def _(k):
        value = partial[1, k] + product(k, 1 - y, core, tail)
        push_twin(0, k).wait_recv()
        to_across[k] = (value + from_twin[0, k].astype(F32)).astype(BF16)
        push_across(k).start()

    @pl.loop(0, 4)
    def _(k):
        to_twin[1, k] = product(k, y, 1 - core, slice(None)).astype(BF16)
        push_twin(1, k).start()

    @pl.loop(0, 4)
    def _(k):
        value = product(k, y, core, slice(None))
        push_twin(1, k).wait_recv()
        partial[0, k] = value + from_twin[1, k].astype(F32)

    @pl.loop(0, 3)
    def _(k):
        push_across(k).wait_recv()
        to_x[k] = (partial[0, k] + from_across[k].astype(F32)).astype(BF16)
        push_owner(k).start()

    push_across(3).wait_recv()
    wgrad[:, window_of(x)] = norm * (partial[0, 3] + from_across[3].astype(F32))
    keep_wgrad(x).start()
    for k, step in enumerate((2, 3, 1)):
        source = (x + step) % 4
        push_owner(k).wait_recv()
        wgrad[:, window_of(source)] = norm * from_x[k].astype(F32)
        keep_wgrad(source).start()

    @pl.loop(0, 4)
    def _(k):
        push_twin(0, k).wait_send()
        push_twin(1, k).wait_send()
        push_across(k).wait_send()

    for k in range(3):
        push_owner(k).wait_send()

    @pl.loop(0, count)
    def _(m):
        for k in range(3):
            push_normed(m, k).wait_send()
            push_s(m, k).wait_send()
        keep_acts(m).wait()
        keep_grads(m).wait()
        for p in range(PIECES):

            @pl.when(section < sections - 1)
            def _():
                push_acts(m, p).wait_send()

            @pl.when(section > 0)
            def _():
                push_grads(m, p).wait_send()

    for k in range(4):
        keep_wgrad(k).wait()


def place(acts_in, grads_in, wgrad_in, acts, grads, wgrad, held, held_wide, in_sems, out_sems):
    parts = 4
    loads, stores = [], []
    arrays = ((acts_in, held.at[0], acts), (grads_in, held.at[1], grads), (wgrad_in, held_wide, wgrad))
    for k, (source, middle, target) in enumerate(arrays):
        step = source.shape[0] // parts
        for i in range(parts):
            rows = slice(i * step, (i + 1) * step)
            loads.append(pltpu.make_async_copy(source.at[rows, :], middle.at[rows, :], in_sems.at[k, i]))
            stores.append(pltpu.make_async_copy(middle.at[rows, :], target.at[rows, :], out_sems.at[k, i]))
    for load in loads:
        load.start()
    for load, store in zip(loads, stores):
        load.wait()
        store.start()
    for store in stores:
        store.wait()


def body(inputs, cotangent, weight, gain):
    micro, tokens, width = inputs.shape
    total = micro * tokens
    share = width // lax.axis_size("dp")
    window = 4 * share
    count = total // CHUNK
    vmem, dma = pltpu.VMEM, pltpu.SemaphoreType.DMA
    anywhere = pl.BlockSpec(memory_space=pl.ANY)
    shapes = (
        jax.ShapeDtypeStruct((total, width), BF16),
        jax.ShapeDtypeStruct((total, width), BF16),
        jax.ShapeDtypeStruct((share, width), F32),
    )
    results = pl.pallas_call(
        kernel,
        out_shape=shapes,
        in_specs=[anywhere] * 3 + [pl.BlockSpec(memory_space=vmem)],
        out_specs=[anywhere] * 3,
        scratch_shapes=[
            vmem((width, width), BF16),
            vmem((width, width), BF16),
            vmem((total, width), BF16),
            vmem((total, width), BF16),
            vmem((total, width), BF16),
            vmem((total, width), BF16),
            vmem((total, width), F32),
            vmem((total, 128), F32),
            vmem((2 * CHUNK, width), F32),
            vmem((total, width), BF16),
            vmem((4 * total, width), BF16),
            vmem((width, 4 * total), BF16),
            vmem((4 * total, window), BF16),
            vmem((2, 4, share, window), F32),
            vmem((2, 4, share, window), BF16),
            vmem((2, 4, share, window), BF16),
            vmem((4, share, window), BF16),
            vmem((4, share, window), BF16),
            vmem((3, share, window), BF16),
            vmem((3, share, window), BF16),
            vmem((share, width), F32),
            dma((PIECES,)),
            dma((3, count)),
            dma((count, PIECES)),
            dma((count, PIECES)),
            dma((count, PIECES)),
            dma((count, PIECES)),
            dma((3, count)),
            dma((3, count)),
            dma((3, count)),
            dma((3, count)),
            dma((2, 4)),
            dma((2, 4)),
            dma((4,)),
            dma((4,)),
            dma((3,)),
            dma((3,)),
        ],
        compiler_params=pltpu.CompilerParams(
            collective_id=0, has_side_effects=True, vmem_limit_bytes=62 * 1024 * 1024
        ),
    )(inputs.reshape(total, width), cotangent.reshape(total, width), weight[0], gain)
    acts, grads, wgrad = pl.pallas_call(
        place,
        out_shape=shapes,
        in_specs=[anywhere] * 3,
        out_specs=[anywhere] * 3,
        scratch_shapes=[vmem((2, total, width), BF16), vmem((share, width), F32), dma((3, 4)), dma((3, 4))],
        compiler_params=pltpu.CompilerParams(vmem_limit_bytes=62 * 1024 * 1024),
    )(*results)
    shape = (1, micro, tokens, width)
    return (acts.reshape(shape), grads.reshape(shape), wgrad[None])


def solution(mesh):
    in_specs = (
        P(None, "dp", None),
        P(None, "dp", None),
        P("section", None, None),
        P("section", None),
    )
    out_specs = (
        P("section", None, "dp", None),
        P("section", None, "dp", None),
        P("section", "dp", None),
    )
    return jax.shard_map(body, mesh=mesh, in_specs=in_specs, out_specs=out_specs, check_vma=False)
```

time: 184 us -> 173 us (0.940)
  Pallas kernels: 184 us -> 172 us
    pallas_call x1, Pallas kernels: 180 us -> 168 us  [body(): pl.pallas_call(kernel, out_shape=shapes, in_specs=[anywhere] * 3 + [pl.Bl...]
where the time goes in v3:
time: 173 us; the launch traced here: 172 us
  Pallas kernels  172 us (99%)
    pallas_call x1, Pallas kernels, body(): pl.pallas_call(kernel, out_shape=shapes, in_specs=[anywhere] * 3 + [pl.Bl...  168 us
    pallas_call x1, Pallas kernels, body(): pl.pallas_call(place, out_shape=shapes, in_specs=[anywhere] * 3, out_spec...  3.86 us

profile of v3, /device:TPU:1, one launch (start us, length us, event | category | flops | bytes accessed | tf_op | source)
XLA Modules:
  0.0 172.5 jit_solution(12314557125163553461)
XLA Ops:
  0.6 167.8 %shard_map.67 = (bf16[256,2560]{1,0:T(8,128)(2,1)}, bf16[256,2560]{1,0:T(8,128)(2,1)}, f32[160,2560]{1,0:T(8,128)}) custom-call(bf16[256,2560]{1,0:T(8,128)(2,1)} %bitcast.7, bf16[256,2560]{1,0:T(8,128)(2,1)} %bitcast.8, bf16[2560,2560]{1,0:T(8,128)(2,1)} %bitcast.6, f32[1,2560]{1,0:T(1,128)} %gain.1), custom_call_target="tpu_custom_call" | custom-call | tf_op jit(solution)/shard_map/pallas_call | solution.py:459
  168.4 3.9 %shard_map.68 = (bf16[256,2560]{1,0:T(8,128)(2,1)}, bf16[256,2560]{1,0:T(8,128)(2,1)}, f32[160,2560]{1,0:T(8,128)}) custom-call(bf16[256,2560]{1,0:T(8,128)(2,1)} %get-tuple-element.9.acts_in, bf16[256,2560]{1,0:T(8,128)(2,1)} %get-tuple-element.10.grads_in, f32[160,2560]{1,0:T(8,128)} %get-tuple-element.11.wgrad_in), custom_call_target="tpu_custom_call" | custom-call | tf_op jit(solution)/shard_map/pallas_call | solution.py:507

commit v4 on v3

--- a/solution.py
+++ b/solution.py
@@ -23,7 +23,7 @@
     x_hbm, d_hbm, w_hbm, gain, acts_out, grads_out, wgrad_out,
     w_v, wt_v, xs, ds_in, acts, grads, pre, rinv, acc, slopes, nx, nt, sx, partial,
     to_twin, from_twin, to_across, from_across, to_x, from_x, wgrad,
-    w_sem, out_sem, f_send, f_recv, b_send, b_recv, n_send, n_recv, s_send, s_recv,
+    w_sem, out_sem, home_sem, f_send, f_recv, b_send, b_recv, n_send, n_recv, s_send, s_recv,
     t_send, t_recv, y_send, y_recv, o_send, o_recv,
 ):
     total, width = xs.shape
@@ -43,8 +43,9 @@
     def at(x_to, y_to, core_to):
         return (section, x_to * 4 + y_to * 2 + core_to)
 
-    after, before = (section + 1, dp), (section - 1, dp)
     twin, across = at(x, y, 1 - core), at(x, 1 - y, core)
+    odd = section % 2 == 1
+    after, before = (section + 1, across[1]), (section - 1, across[1])
     steps = (1, 3, 2)
     others = [(x + step) % 4 for step in steps]
 
@@ -77,7 +78,7 @@
     def fetch_d(m):
         for p in range(PIECES):
             here = (rows_of(m), cols(p))
-            local(d_hbm.at[here], ds_in.at[here], b_recv.at[m, p]).start()
+            yield remote(d_hbm.at[here], ds_in.at[here], f_send.at[m, p], b_recv.at[m, p], across)
 
     def fetch_w(p):
         return local(w_hbm.at[cols(p), :], w_v.at[cols(p), :], w_sem.at[p])
@@ -103,11 +104,24 @@
             at(others[k], y, core),
         )
 
-    def keep_acts(m):
-        return local(acts.at[rows_of(m), :], acts_out.at[rows_of(m), :], out_sem.at[0, m])
-
-    def keep_grads(m):
-        return local(grads.at[rows_of(m), :], grads_out.at[rows_of(m), :], out_sem.at[1, m])
+    def keep(k, m):
+        source, target = ((acts, acts_out), (grads, grads_out))[k]
+        return local(source.at[rows_of(m), :], target.at[rows_of(m), :], out_sem.at[k, m])
+
+    def home(k, m):
+        source, target = ((acts, acts_out), (grads, grads_out))[k]
+        return remote(
+            source.at[rows_of(m), :], target.at[rows_of(m), :], out_sem.at[k, m], home_sem.at[k, m], across
+        )
+
+    def leave(k, m):
+        @pl.when(odd)
+        def _():
+            home(k, m).start()
+
+        @pl.when(jnp.logical_not(odd))
+        def _():
+            keep(k, m).start()
 
     @pl.when(first)
     def _():
@@ -119,12 +133,6 @@
     @pl.when(first)
     def _():
         fetch_x(1)
-
-    @pl.when(last)
-    def _():
-        @pl.loop(0, count)
-        def _(m):
-            fetch_d(m)
 
     barrier = pltpu.get_barrier_semaphore()
     for device in [twin, across] + [at(other, y, core) for other in others]:
@@ -139,6 +147,13 @@
         pl.semaphore_signal(barrier, inc=1, device_id=after, device_id_type=MESH)
 
     pl.semaphore_wait(barrier, 5 + (section > 0).astype(jnp.int32) + (section < sections - 1).astype(jnp.int32))
+
+    @pl.when(last)
+    def _():
+        @pl.loop(0, count)
+        def _(m):
+            for copy in fetch_d(m):
+                copy.start()
 
     def turn_weight():
         tile = 256
@@ -234,11 +249,11 @@
         for p in range(PIECES):
             nx[slot(m, x, n), cols(p)] = (xs[rows, cols(p)].astype(F32) * r * gain[:, cols(p)]).astype(BF16)
         for i in range(n):
-            keep_acts(m + i).start()
+            leave(0, m + i)
             for k in range(3):
                 push_normed(m + i, k).start()
 
-    def backward(m, n):
+    def backward(m, n, eager=False):
         rows = rows_of(m, n)
         taken = n * CHUNK
         dots = None
@@ -254,13 +269,18 @@
             slopes[rows, cols(p)] = s
             term = lane_sum(s.astype(F32) * a)
             dots = term if dots is None else dots + term
-            add_product(s, wt_v, p, taken)
+            if not eager:
+                add_product(s, wt_v, p, taken)
 
         def share_s():
             for i in range(n):
                 for k in range(3):
                     push_s(m + i, k).start()
 
+        if eager:
+            share_s()
+            for p in range(PIECES):
+                add_product(slopes[rows, cols(p)], wt_v, p, taken)
         r = rinv[rows, :1]
         scale = r * r * (jnp.sum(dots, -1, keepdims=True) * (1.0 / width))
         for block in BLOCKS:
@@ -272,28 +292,31 @@
                 )
                 grads[rows, cols(p)] = out.astype(BF16)
 
-            @pl.when(section > 0)
-            def _():
-                for i in range(n):
-                    for p in block:
-                        push_grads(m + i, p).start()
-
-        share_s()
+            if not eager:
+
+                @pl.when(section > 0)
+                def _():
+                    for i in range(n):
+                        for p in block:
+                            push_grads(m + i, p).start()
+
+        if not eager:
+            share_s()
         sx[slot(m, x, n), :] = slopes[rows, window_of(x)]
         for i in range(n):
-            keep_grads(m + i).start()
+            leave(1, m + i)
 
     behind = sections - 1 - section
     paired = behind < PAIRED
     pairs = (count - 2 * SINGLES) // 2
     lag = jnp.where(paired, AHEAD * behind, count)
 
-    def visit(step, paired, work, skip):
+    def visit(step, work, skip, spare):
         inside = jnp.logical_and(step >= SINGLES, step < SINGLES + pairs)
         two = jnp.logical_and(paired, inside)
         start = jnp.where(step < SINGLES, step, jnp.where(inside, 2 * step - SINGLES, step + pairs))
         start = jnp.where(paired, start, step)
-        active = jnp.logical_and(step >= skip, step < jnp.where(paired, pairs + 2 * SINGLES, count))
+        active = jnp.logical_and(step >= skip, step < jnp.where(paired, pairs + 2 * SINGLES, count) - spare)
 
         @pl.when(jnp.logical_and(active, two))
         def _():
@@ -309,14 +332,18 @@
 
     @pl.loop(0, 2 * count)
     def _(i):
-        visit(i, paired, forward, first.astype(jnp.int32))
+        visit(i, forward, first.astype(jnp.int32), 0)
 
         @pl.when(jnp.logical_and(i == count - 1, jnp.logical_not(early)))
         def _():
             turn_weight()
             turn_normed()
 
-        visit(i - lag, paired, backward, 0)
+        visit(i - lag, backward, 0, first.astype(jnp.int32))
+
+    @pl.when(first)
+    def _():
+        backward(count - 1, 1, eager=True)
 
     @pl.when(early)
     def _():
@@ -378,6 +405,36 @@
         value = product(k, y, core, slice(None))
         push_twin(1, k).wait_recv()
         partial[0, k] = value + from_twin[1, k].astype(F32)
+
+    @pl.loop(0, count)
+    def _(m):
+        for k in range(3):
+            push_normed(m, k).wait_send()
+            push_s(m, k).wait_send()
+        for k in range(2):
+
+            @pl.when(odd)
+            def _():
+                home(k, m).wait()
+
+            @pl.when(jnp.logical_not(odd))
+            def _():
+                keep(k, m).wait()
+
+        @pl.when(last)
+        def _():
+            for copy in fetch_d(m):
+                copy.wait_send()
+
+        for p in range(PIECES):
+
+            @pl.when(section < sections - 1)
+            def _():
+                push_acts(m, p).wait_send()
+
+            @pl.when(section > 0)
+            def _():
+                push_grads(m, p).wait_send()
 
     @pl.loop(0, 3)
     def _(k):
@@ -402,23 +459,6 @@
 
     for k in range(3):
         push_owner(k).wait_send()
-
-    @pl.loop(0, count)
-    def _(m):
-        for k in range(3):
-            push_normed(m, k).wait_send()
-            push_s(m, k).wait_send()
-        keep_acts(m).wait()
-        keep_grads(m).wait()
-        for p in range(PIECES):
-
-            @pl.when(section < sections - 1)
-            def _():
-                push_acts(m, p).wait_send()
-
-            @pl.when(section > 0)
-            def _():
-                push_grads(m, p).wait_send()
 
     for k in range(4):
         keep_wgrad(k).wait()
@@ -485,6 +525,7 @@
             vmem((share, width), F32),
             dma((PIECES,)),
             dma((3, count)),
+            dma((2, count)),
             dma((count, PIECES)),
             dma((count, PIECES)),
             dma((count, PIECES)),

time: 173 us -> 169 us (0.977); the launches traced: 172 us -> 166 us
  Pallas kernels: 172 us -> 166 us
    pallas_call x1, Pallas kernels: 168 us -> 162 us  [body(): pl.pallas_call(kernel, out_shape=shapes, in_specs=[anywhere] * 3 + [pl.Bl...]
where the time goes in v4:
time: 169 us; the launch traced here: 166 us
  Pallas kernels  166 us (98%)
    pallas_call x1, Pallas kernels, body(): pl.pallas_call(kernel, out_shape=shapes, in_specs=[anywhere] * 3 + [pl.Bl...  162 us
    pallas_call x1, Pallas kernels, body(): pl.pallas_call(place, out_shape=shapes, in_specs=[anywhere] * 3, out_spec...  3.86 us

profile of v4, /device:TPU:1, one launch (start us, length us, event | category | flops | bytes accessed | tf_op | source)
XLA Modules:
  0.0 166.4 jit_solution(16655291162787251857)
XLA Ops:
  0.6 161.7 %shard_map.67 = (bf16[256,2560]{1,0:T(8,128)(2,1)}, bf16[256,2560]{1,0:T(8,128)(2,1)}, f32[160,2560]{1,0:T(8,128)}) custom-call(bf16[256,2560]{1,0:T(8,128)(2,1)} %bitcast.7, bf16[256,2560]{1,0:T(8,128)(2,1)} %bitcast.8, bf16[2560,2560]{1,0:T(8,128)(2,1)} %bitcast.6, f32[1,2560]{1,0:T(1,128)} %gain.1), custom_call_target="tpu_custom_call" | custom-call | tf_op jit(solution)/shard_map/pallas_call | solution.py:499
  162.3 3.9 %shard_map.68 = (bf16[256,2560]{1,0:T(8,128)(2,1)}, bf16[256,2560]{1,0:T(8,128)(2,1)}, f32[160,2560]{1,0:T(8,128)}) custom-call(bf16[256,2560]{1,0:T(8,128)(2,1)} %get-tuple-element.9.acts_in, bf16[256,2560]{1,0:T(8,128)(2,1)} %get-tuple-element.10.grads_in, f32[160,2560]{1,0:T(8,128)} %get-tuple-element.11.wgrad_in), custom_call_target="tpu_custom_call" | custom-call | tf_op jit(solution)/shard_map/pallas_call | solution.py:548

commit v5 on v4

--- a/solution.py
+++ b/solution.py
@@ -10,12 +10,13 @@
 BF16, F32 = jnp.bfloat16, jnp.float32
 
 CHUNK = 16
-PIECES = 5
+EDGES = (0, 256, 768, 1280, 1792, 2304, 2560)
+PIECES = len(EDGES) - 1
 GROUP = 64
 PAIRED = 2
 SINGLES = 2
 AHEAD = 3
-BLOCKS = ((0, 1), (2, 3, 4))
+BLOCKS = ((0, 1), (2, 3, 4, 5))
 PADDED = 128
 
 
@@ -28,7 +29,6 @@
 ):
     total, width = xs.shape
     count = total // CHUNK
-    piece = width // PIECES
     window = sx.shape[1]
     share = wgrad.shape[0]
     per_group = GROUP // CHUNK
@@ -58,7 +58,7 @@
         )
 
     def cols(p):
-        return slice(p * piece, (p + 1) * piece)
+        return slice(EDGES[p], EDGES[p + 1])
 
     def rows_of(m, n=1):
         return pl.ds(pl.multiple_of(m * CHUNK, CHUNK), n * CHUNK)
@@ -197,7 +197,7 @@
     def add_product(lhs, rhs, p, taken):
         tile = 512
         if taken > CHUNK:
-            lhs = jnp.concatenate([lhs, jnp.zeros((PADDED - taken, piece), BF16)], 0)
+            lhs = jnp.concatenate([lhs, jnp.zeros((PADDED - taken, lhs.shape[1]), BF16)], 0)
         for j in range(0, width, tile):
             term = jnp.dot(lhs, rhs[cols(p), j : j + tile], preferred_element_type=F32)[:taken]
             if p == 0:
@@ -372,11 +372,18 @@
     def push_twin(half, k):
         return remote(to_twin.at[half, k], from_twin.at[half, k], t_send.at[half, k], t_recv.at[half, k], twin)
 
-    def push_across(k):
-        return remote(to_across.at[k], from_across.at[k], y_send.at[k], y_recv.at[k], across)
-
-    def push_owner(k):
-        return remote(to_x.at[k], from_x.at[k], o_send.at[k], o_recv.at[k], at(owner(k), y, core))
+    half = share // 2
+
+    def half_of(h):
+        return pl.ds(pl.multiple_of(h * half, 16), half)
+
+    def push_across(k, h):
+        here = (k, half_of(h))
+        return remote(to_across.at[here], from_across.at[here], y_send.at[k, h], y_recv.at[k, h], across)
+
+    def push_owner(k, h):
+        here = (k, half_of(h))
+        return remote(to_x.at[here], from_x.at[here], o_send.at[k, h], o_recv.at[k, h], at(owner(k), y, core))
 
     def keep_wgrad(source):
         return local(wgrad.at[:, window_of(source)], wgrad_out.at[:, window_of(source)], out_sem.at[2, source])
@@ -393,7 +400,8 @@
         value = partial[1, k] + product(k, 1 - y, core, tail)
         push_twin(0, k).wait_recv()
         to_across[k] = (value + from_twin[0, k].astype(F32)).astype(BF16)
-        push_across(k).start()
+        for h in range(2):
+            push_across(k, h).start()
 
     @pl.loop(0, 4)
     def _(k):
@@ -438,16 +446,19 @@
 
     @pl.loop(0, 3)
     def _(k):
-        push_across(k).wait_recv()
-        to_x[k] = (partial[0, k] + from_across[k].astype(F32)).astype(BF16)
-        push_owner(k).start()
-
-    push_across(3).wait_recv()
+        for h in range(2):
+            push_across(k, h).wait_recv()
+            to_x[k, half_of(h)] = (partial[0, k, half_of(h)] + from_across[k, half_of(h)].astype(F32)).astype(BF16)
+            push_owner(k, h).start()
+
+    for h in range(2):
+        push_across(3, h).wait_recv()
     wgrad[:, window_of(x)] = norm * (partial[0, 3] + from_across[3].astype(F32))
     keep_wgrad(x).start()
     for k, step in enumerate((2, 3, 1)):
         source = (x + step) % 4
-        push_owner(k).wait_recv()
+        for h in range(2):
+            push_owner(k, h).wait_recv()
         wgrad[:, window_of(source)] = norm * from_x[k].astype(F32)
         keep_wgrad(source).start()
 
@@ -455,10 +466,12 @@
     def _(k):
         push_twin(0, k).wait_send()
         push_twin(1, k).wait_send()
-        push_across(k).wait_send()
+        for h in range(2):
+            push_across(k, h).wait_send()
 
     for k in range(3):
-        push_owner(k).wait_send()
+        for h in range(2):
+            push_owner(k, h).wait_send()
 
     for k in range(4):
         keep_wgrad(k).wait()
@@ -536,10 +549,10 @@
             dma((3, count)),
             dma((2, 4)),
             dma((2, 4)),
-            dma((4,)),
-            dma((4,)),
-            dma((3,)),
-            dma((3,)),
+            dma((4, 2)),
+            dma((4, 2)),
+            dma((3, 2)),
+            dma((3, 2)),
         ],
         compiler_params=pltpu.CompilerParams(
             collective_id=0, has_side_effects=True, vmem_limit_bytes=62 * 1024 * 1024

time: 169 us -> 168 us (level)
  no operation moved by 1% of the time
where the time goes in v5:
time: 168 us; the launch traced here: 167 us
  Pallas kernels  166 us (99%)
    pallas_call x1, Pallas kernels, body(): pl.pallas_call(kernel, out_shape=shapes, in_specs=[anywhere] * 3 + [pl.Bl...  162 us
    pallas_call x1, Pallas kernels, body(): pl.pallas_call(place, out_shape=shapes, in_specs=[anywhere] * 3, out_spec...  3.86 us

profile of v5, /device:TPU:1, one launch (start us, length us, event | category | flops | bytes accessed | tf_op | source)
XLA Modules:
  0.0 166.8 jit_solution(7463716375390129854)
XLA Ops:
  0.6 162.2 %shard_map.67 = (bf16[256,2560]{1,0:T(8,128)(2,1)}, bf16[256,2560]{1,0:T(8,128)(2,1)}, f32[160,2560]{1,0:T(8,128)}) custom-call(bf16[256,2560]{1,0:T(8,128)(2,1)} %bitcast.7, bf16[256,2560]{1,0:T(8,128)(2,1)} %bitcast.8, bf16[2560,2560]{1,0:T(8,128)(2,1)} %bitcast.6, f32[1,2560]{1,0:T(1,128)} %gain.1), custom_call_target="tpu_custom_call" | custom-call | tf_op jit(solution)/shard_map/pallas_call | solution.py:512
  162.8 3.9 %shard_map.68 = (bf16[256,2560]{1,0:T(8,128)(2,1)}, bf16[256,2560]{1,0:T(8,128)(2,1)}, f32[160,2560]{1,0:T(8,128)}) custom-call(bf16[256,2560]{1,0:T(8,128)(2,1)} %get-tuple-element.9.acts_in, bf16[256,2560]{1,0:T(8,128)(2,1)} %get-tuple-element.10.grads_in, f32[160,2560]{1,0:T(8,128)} %get-tuple-element.11.wgrad_in), custom_call_target="tpu_custom_call" | custom-call | tf_op jit(solution)/shard_map/pallas_call | solution.py:561

commit v6 on v5

--- a/solution.py
+++ b/solution.py
@@ -390,18 +390,25 @@
 
     norm = float(4096) ** (-0.5)
 
-    @pl.loop(0, 4)
-    def _(k):
+    def offer(k):
         to_twin[0, k] = (partial[0, k] + product(k, 1 - y, 1 - core, tail)).astype(BF16)
         push_twin(0, k).start()
 
-    @pl.loop(0, 4)
-    def _(k):
+    def hand_on(k):
         value = partial[1, k] + product(k, 1 - y, core, tail)
         push_twin(0, k).wait_recv()
         to_across[k] = (value + from_twin[0, k].astype(F32)).astype(BF16)
         for h in range(2):
             push_across(k, h).start()
+
+    pl.loop(0, 2)(offer)
+
+    @pl.loop(0, 2)
+    def _(k):
+        hand_on(k)
+        offer(k + 2)
+
+    pl.loop(2, 4)(hand_on)
 
     @pl.loop(0, 4)
     def _(k):

time: 168 us -> 168 us (level)
  no operation moved by 1% of the time
where the time goes in v6:
time: 168 us; the launch traced here: 167 us
  Pallas kernels  166 us (99%)
    pallas_call x1, Pallas kernels, body(): pl.pallas_call(kernel, out_shape=shapes, in_specs=[anywhere] * 3 + [pl.Bl...  162 us
    pallas_call x1, Pallas kernels, body(): pl.pallas_call(place, out_shape=shapes, in_specs=[anywhere] * 3, out_spec...  3.86 us

profile of v6, /device:TPU:1, one launch (start us, length us, event | category | flops | bytes accessed | tf_op | source)
XLA Modules:
  0.0 167.0 jit_solution(7564843976682120008)
XLA Ops:
  0.6 162.4 %shard_map.67 = (bf16[256,2560]{1,0:T(8,128)(2,1)}, bf16[256,2560]{1,0:T(8,128)(2,1)}, f32[160,2560]{1,0:T(8,128)}) custom-call(bf16[256,2560]{1,0:T(8,128)(2,1)} %bitcast.7, bf16[256,2560]{1,0:T(8,128)(2,1)} %bitcast.8, bf16[2560,2560]{1,0:T(8,128)(2,1)} %bitcast.6, f32[1,2560]{1,0:T(1,128)} %gain.1), custom_call_target="tpu_custom_call" | custom-call | tf_op jit(solution)/shard_map/pallas_call | solution.py:519
  163.0 3.9 %shard_map.68 = (bf16[256,2560]{1,0:T(8,128)(2,1)}, bf16[256,2560]{1,0:T(8,128)(2,1)}, f32[160,2560]{1,0:T(8,128)}) custom-call(bf16[256,2560]{1,0:T(8,128)(2,1)} %get-tuple-element.9.acts_in, bf16[256,2560]{1,0:T(8,128)(2,1)} %get-tuple-element.10.grads_in, f32[160,2560]{1,0:T(8,128)} %get-tuple-element.11.wgrad_in), custom_call_target="tpu_custom_call" | custom-call | tf_op jit(solution)/shard_map/pallas_call | solution.py:568
